TPU v7x, 32 devices: a whole 2x2x4 slice. The times are simulated.
32 devices in a mesh: inline: 2 (over x), xline: 16 (over z, y, core).
Axes of the slice: x: 2, y: 2, z: 4, core: 2. Of those that a mesh axis runs over, the one named last changes fastest.
Arguments:
- traces: float32 [16, 256, 1024], P('inline', 'xline'), may hold values from -6 to 6
- filters: float32 [2, 512, 81], replicated, may hold values from -0.6 to 0.6
Outputs:
- denoised: float32 [16, 256, 1024], P('inline', 'xline')
All inputs are finite; a program needn't handle non-finite values.
Results may differ from a plain program's by a relative error of at most 0.00007.
Values sent between devices are 32-bit elements; how exact they have to be, the bound alone decides.
A program may use at most 64 MiB of HBM per device.

v0:
```python
import math

import jax
import jax.numpy as jnp
from jax import lax
from jax.sharding import PartitionSpec as P


def extended(block, sides, width):
    for axis, dim in sides:
        count = lax.axis_size(axis)
        forward = [(i, i + 1) for i in range(count - 1)]
        backward = [(target, source) for source, target in forward]
        low = lax.ppermute(
            lax.slice_in_dim(block, block.shape[dim] - width, None, axis=dim), axis, forward
        )
        high = lax.ppermute(lax.slice_in_dim(block, 0, width, axis=dim), axis, backward)
        block = jnp.concatenate([low, block, high], axis=dim)
    return block


def tables(samples, frequencies):
    time_index = jnp.arange(samples, dtype=jnp.int32)
    bin_index = jnp.arange(frequencies, dtype=jnp.int32)
    phase_steps = time_index[:, None] * bin_index[None, :] % samples
    phase = phase_steps.astype(jnp.float32) * (2.0 * math.pi / samples)
    cosine = jnp.cos(phase)
    sine = jnp.sin(phase)
    forward_table = jnp.stack((cosine, -sine), axis=1)
    weights = jnp.where(bin_index == 0, 1.0, 2.0).astype(jnp.float32) / samples
    inverse_table = jnp.stack((weights[:, None] * cosine.T, -weights[:, None] * sine.T), axis=0)
    return (forward_table, inverse_table)


def correlate(padded, filter_taps, row_count, col_count):
    windows = jnp.stack(
        [padded[:, :, :, shift_col : shift_col + col_count] for shift_col in range(9)], axis=0
    )
    tap_grid = filter_taps.reshape(2, filter_taps.shape[1], 9, 9)
    total_real = None
    total_imag = None
    for shift_row in range(9):
        tap_row = jnp.transpose(tap_grid[:, :, shift_row, :], (2, 0, 1))
        weight = tap_row[:, :, None, :, None]
        weight_real = weight[:, 0]
        weight_imag = weight[:, 1]
        piece = windows[:, :, shift_row : shift_row + row_count]
        piece_real = piece[:, 0]
        piece_imag = piece[:, 1]
        add_real = jnp.sum(weight_real * piece_real - weight_imag * piece_imag, axis=0)
        add_imag = jnp.sum(weight_real * piece_imag + weight_imag * piece_real, axis=0)
        if total_real is None:
            total_real = add_real
            total_imag = add_imag
        else:
            total_real = total_real + add_real
            total_imag = total_imag + add_imag
    return jnp.stack((total_real, total_imag), axis=0)


def per_device(traces, filters):
    count_inline, count_xline, samples = traces.shape
    frequencies = filters.shape[1]
    forward_table, inverse_table = tables(samples, frequencies)
    highest = lax.Precision.HIGHEST
    spectrum = jnp.einsum("ixt,tpf->pifx", traces, forward_table, precision=highest)
    spectral_slab = lax.all_to_all(spectrum, "xline", split_axis=2, concat_axis=3, tiled=True)
    group_bins = spectral_slab.shape[2]
    first_bin = lax.axis_index("xline") * group_bins
    filter_taps = lax.dynamic_slice_in_dim(filters, first_bin, group_bins, 1)
    padded = extended(spectral_slab, (("inline", 1),), 4)
    padded = jnp.pad(padded, ((0, 0), (0, 0), (0, 0), (4, 4)))
    result = correlate(padded, filter_taps, spectral_slab.shape[1], spectral_slab.shape[3])
    returned = lax.all_to_all(result, "xline", split_axis=3, concat_axis=2, tiled=True)
    denoised = jnp.einsum("pifx,pft->ixt", returned, inverse_table, precision=highest)
    return denoised


def solution(mesh):
    return jax.shard_map(
        per_device,
        mesh=mesh,
        in_specs=(P("inline", "xline", None), P()),
        out_specs=P("inline", "xline", None),
        check_vma=False,
    )
```

profile of v0, /device:TPU:1, one launch (start us, length us, event | category | flops | bytes accessed | tf_op | source)
XLA Modules:
  0.0 118.4 jit_solution(16982166092393978417)
XLA Ops:
  0.0 8.2 %sine_negate_fusion = (f32[1024,1,512]{2,0,1:T(8,128)S(1)}, f32[1024,1,512]{2,0,1:T(8,128)S(1)}) fusion(), kind=kLoop, calls=%fused_computation.68 | loop fusion | flops 7864320 | bytes 4194304 | tf_op jit(solution)/shard_map/neg | solution.py:29
  8.3 2.4 %fusion.19 = f32[2,8,512,16]{2,3,1,0:T(8,128)S(1)} fusion(f32[1024,1,512]{2,0,1:T(8,128)S(1)} %get-tuple-element.64, f32[1024,1,512]{2,0,1:T(8,128)S(1)} %get-tuple-element.65, f32[8,16,1024]{2,1,0:T(8,128)S(1)} %copy-done), kind=kOutput, calls=%fused_computation.74 | convolution fusion | flops 1611661312 | bytes 5242880 | tf_op jit(solution)/shard_map/ixt,tpf->pifx/dot_general | solution.py:66
  10.7 3.8 %copy.33 = f32[2,8,512,16]{3,1,0,2:T(8,128)} copy(f32[2,8,512,16]{2,3,1,0:T(8,128)S(1)} %fusion.19) | data formatting | bytes 1048576 | tf_op jit(solution)/shard_map/ixt,tpf->pifx/transpose | solution.py:66
  14.5 4.2 %reshape.353 = f32[16,1,8192]{2,1,0:T(1,128)} reshape(f32[512,2,8,16]{3,2,1,0:T(8,128)} %bitcast.309) | data formatting | bytes 1048576
  18.7 7.4 %all-to-all-start = ((f32[16,1,8192]{2,1,0:T(1,128)}), f32[16,1,8192]{2,1,0:T(1,128)S(1)}, u32[]{:S(2)}, u32[]{:S(2)}) async-start(f32[16,1,8192]{2,1,0:T(1,128)} %reshape.353), calls=%async_computation | async-start | bytes 1048576 | tf_op jit(solution)/shard_map/all_to_all | solution.py:67
  26.0 1.0 constant_dynamic-slice_fusion
  27.2 12.9 %all-to-all-done = f32[16,1,8192]{2,1,0:T(1,128)S(1)} async-done(((f32[16,1,8192]{2,1,0:T(1,128)}), f32[16,1,8192]{2,1,0:T(1,128)S(1)}, u32[]{:S(2)}, u32[]{:S(2)}) %all-to-all-start) | async-done | bytes 524320 | tf_op jit(solution)/shard_map/all_to_all | solution.py:67
  40.6 1.9 %reduce = f32[16,8192]{1,0:T(8,128)S(1)} reduce(f32[16,1,8192]{2,1,0:T(1,128)S(1)} %all-to-all-done, f32[]{:T(128)} %broadcast.239), dimensions={1}, to_apply=%all_to_all.26.reduce_sub_computation | reduce | bytes 1048580 | tf_op jit(solution)/shard_map/all_to_all | solution.py:67
  42.5 2.8 %reshape.354 = f32[512,2,8,16]{3,2,1,0:T(8,128)} reshape(f32[16,8192]{1,0:T(8,128)S(1)} %reduce) | data formatting | bytes 1048576
  45.2 2.8 %copy.34 = f32[2,8,16,32,16]{3,4,2,1,0:T(8,128)S(1)} copy(f32[2,8,16,32,16]{4,1,0,3,2:T(8,128)} %bitcast.310) | data formatting | bytes 1048576 | tf_op jit(solution)/shard_map/all_to_all | solution.py:67
  48.1 1.5 %fusion.41 = (f32[2,4,32,256]{2,3,1,0:T(8,128)}, f32[2,4,32,256]{2,3,1,0:T(8,128)}) fusion(f32[2,8,32,256]{2,3,1,0:T(8,128)S(1)} %bitcast.307), kind=kLoop, calls=%fused_computation.131 | loop fusion | bytes 1048576 | tf_op jit(solution)/shard_map/slice | solution.py:15
  49.6 2.3 %copy.35 = f32[2,4,32,256]{3,2,1,0:T(8,128)} copy(f32[2,4,32,256]{2,3,1,0:T(8,128)} %get-tuple-element.35) | data formatting | bytes 524288 | tf_op jit(solution)/shard_map/slice | solution.py:15
  51.8 3.1 %collective-permute-start = (f32[2,4,32,256]{3,2,1,0:T(8,128)}, f32[2,4,32,256]{3,2,1,0:T(8,128)S(1)}, u32[]{:S(2)}, u32[]{:S(2)}) collective-permute-start(f32[2,4,32,256]{3,2,1,0:T(8,128)} %copy.35), channel_id=1, source_target_pairs={{0,16},{1,17},{2,18},{3,19},{4,20},{5,21},{6,22},{7,23},{8,24},{9,... | collective-permute-start | bytes 786440 | tf_op jit(solution)/shard_map/ppermute | solution.py:14
  55.0 2.2 %copy.36 = f32[2,4,32,256]{3,2,1,0:T(8,128)} copy(f32[2,4,32,256]{2,3,1,0:T(8,128)} %get-tuple-element.36) | data formatting | bytes 524288 | tf_op jit(solution)/shard_map/slice | solution.py:17
  57.2 1.3 %collective-permute-start.1 = (f32[2,4,32,256]{3,2,1,0:T(8,128)}, f32[2,4,32,256]{3,2,1,0:T(8,128)}, u32[]{:S(2)}, u32[]{:S(2)}) collective-permute-start(f32[2,4,32,256]{3,2,1,0:T(8,128)} %copy.36), channel_id=1, source_target_pairs={{16,0},{17,1},{18,2},{19,3},{20,4},{21,5},{22,6},{23,7},{24,8},{25... | collective-permute-start | bytes 786440 | tf_op jit(solution)/shard_map/ppermute | solution.py:17
  59.3 1.2 collective-permute-done
  60.4 6.0 %collective-permute-done.1 = f32[2,4,32,256]{3,2,1,0:T(8,128)} collective-permute-done((f32[2,4,32,256]{3,2,1,0:T(8,128)}, f32[2,4,32,256]{3,2,1,0:T(8,128)}, u32[]{:S(2)}, u32[]{:S(2)}) %collective-permute-start.1) | collective-permute-done | bytes 262176 | tf_op jit(solution)/shard_map/ppermute | solution.py:17
  66.5 1.0 pad_maximum_fusion
  68.9 1.0 bitcast_dynamic-update-slice_fusion
  71.3 2.6 %subtract_reduce_fusion.8 = (f32[8,32,256]{2,1,0:T(8,128)S(1)}, f32[8,32,256]{2,1,0:T(8,128)S(1)}, f32[8,32,256]{2,1,0:T(8,128)S(1)}, f32[8,32,256]{2,1,0:T(8,12...) fusion(f32[9,2,16,32,256]{4,3,2,1,0:T(8,128)S(1)} %fusion.35, f32[9,32]{1,0:T(8,128)S(1)} %bitcast.326, ...), kind=kLoop, calls=%fused_computation.57 | loop fusion | flops 13762560 | bytes 15735552 | tf_op jit(solution)/shard_map/reduce_sum | solution.py:50
  73.9 2.4 %subtract_reduce_fusion.7 = (f32[8,32,256]{2,1,0:T(8,128)S(1)}, f32[8,32,256]{2,1,0:T(8,128)S(1)}, f32[8,32,256]{2,1,0:T(8,128)S(1)}, f32[8,32,256]{2,1,0:T(8,12...) fusion(f32[9,2,16,32,256]{4,3,2,1,0:T(8,128)S(1)} %fusion.35, f32[9,32]{1,0:T(8,128)S(1)} %bitcast.327, ...), kind=kLoop, calls=%fused_computation.56 | loop fusion | flops 13762560 | bytes 15735552 | tf_op jit(solution)/shard_map/reduce_sum | solution.py:50
  76.3 2.4 %subtract_reduce_fusion.6 = (f32[8,32,256]{2,1,0:T(8,128)S(1)}, f32[8,32,256]{2,1,0:T(8,128)S(1)}, f32[8,32,256]{2,1,0:T(8,128)S(1)}, f32[8,32,256]{2,1,0:T(8,12...) fusion(f32[9,2,16,32,256]{4,3,2,1,0:T(8,128)S(1)} %fusion.35, f32[9,32]{1,0:T(8,128)S(1)} %get-tuple-element.74, ...), kind=kLoop, calls=%fused_computation.55 | loop fusion | flops 13762560 | bytes 15735552 | tf_op jit(solution)/shard_map/reduce_sum | solution.py:50
  79.1 1.3 %copy.47 = f32[2,8,32,256]{2,1,0,3:T(8,128)S(1)} copy(f32[2,8,32,256]{3,2,1,0:T(8,128)S(1)} %pad_maximum_fusion.1) | data formatting | bytes 1048576 | tf_op jit(solution)/shard_map/stack | solution.py:58
  80.4 1.7 %reshape.355 = f32[16,1,8192]{2,1,0:T(1,128)} reshape(f32[256,2,8,32]{3,2,1,0:T(8,128)S(1)} %bitcast.311) | data formatting | bytes 1048576
  82.1 5.9 %all-to-all-start.1 = ((f32[16,1,8192]{2,1,0:T(1,128)}), f32[16,1,8192]{2,1,0:T(1,128)}, u32[]{:S(2)}, u32[]{:S(2)}) async-start(f32[16,1,8192]{2,1,0:T(1,128)} %reshape.355), calls=%async_computation.1 | async-start | bytes 1048576 | tf_op jit(solution)/shard_map/all_to_all | solution.py:74
  88.1 9.2 %sine_multiply_fusion = (f32[1,512,1024]{2,1,0:T(8,128)S(1)}, f32[1,512,1024]{2,1,0:T(8,128)}) fusion(f32[512]{0:T(512)S(1)} %fusion.38, f32[512]{0:T(512)S(1)} %select_multiply_fusion), kind=kLoop, calls=%fused_computation.64 | loop fusion | flops 8388608 | bytes 4198400 | tf_op jit(solution)/shard_map/mul | solution.py:31
  97.4 4.9 %all-to-all-done.1 = f32[16,1,8192]{2,1,0:T(1,128)} async-done(((f32[16,1,8192]{2,1,0:T(1,128)}), f32[16,1,8192]{2,1,0:T(1,128)}, u32[]{:S(2)}, u32[]{:S(2)}) %all-to-all-start.1) | async-done | bytes 524320 | tf_op jit(solution)/shard_map/all_to_all | solution.py:74
  102.3 2.9 %reduce.1 = f32[16,8192]{1,0:T(8,128)S(1)} reduce(f32[16,1,8192]{2,1,0:T(1,128)} %all-to-all-done.1, f32[]{:T(128)} %broadcast.239), dimensions={1}, to_apply=%all_to_all.30.reduce_sub_computation | reduce | bytes 1048580 | tf_op jit(solution)/shard_map/all_to_all | solution.py:74
  105.2 2.0 %reshape.356 = f32[256,2,8,32]{3,2,1,0:T(8,128)} reshape(f32[16,8192]{1,0:T(8,128)S(1)} %reduce.1) | data formatting | bytes 1048576
  107.2 4.1 %copy.49 = f32[2,8,16,32,16]{3,2,4,0,1:T(8,128)} copy(f32[2,8,16,32,16]{3,1,0,4,2:T(8,128)} %bitcast.312) | data formatting | bytes 1048576 | tf_op jit(solution)/shard_map/all_to_all | solution.py:74
  111.3 2.3 %all_to_all.33 = f32[2,8,512,16]{2,3,0,1:T(8,128)S(1)} reshape(f32[2,8,16,32,16]{3,2,4,0,1:T(8,128)} %copy.49) | data formatting | bytes 1048576 | tf_op jit(solution)/shard_map/all_to_all | solution.py:74
  113.6 4.8 %fusion.18 = f32[8,16,1024]{2,1,0:T(8,128)} fusion(f32[2,8,512,16]{2,3,0,1:T(8,128)S(1)} %all_to_all.33, f32[1,512,1024]{2,1,0:T(8,128)S(1)} %get-tuple-element.76, f32[1,512,1024]{2,1,0:T(8,128)} %get-tuple-element.77), kind=kOutput, calls=%fused_computation.73 | convolution fusion | flops 1611661312 | bytes 5242880 | tf_op jit(solution)/shard_map/pifx,pft->ixt/dot_general | solution.py:75
  (40 shorter events, 4.3 us)
Async XLA Ops:
  0.0 8.2 %copy-start = (f32[8,16,1024]{2,1,0:T(8,128)S(1)}, f32[8,16,1024]{2,1,0:T(8,128)}, u32[]{:S(2)}) copy-start(f32[8,16,1024]{2,1,0:T(8,128)} %param.2) | copy-start | bytes 1572868
  18.7 21.4 %all-to-all-start = ((f32[16,1,8192]{2,1,0:T(1,128)}), f32[16,1,8192]{2,1,0:T(1,128)S(1)}, u32[]{:S(2)}, u32[]{:S(2)}) async-start(f32[16,1,8192]{2,1,0:T(1,128)} %reshape.353), calls=%async_computation | async-start | bytes 1048576 | tf_op jit(solution)/shard_map/all_to_all | solution.py:67
  51.8 8.6 %collective-permute-start = (f32[2,4,32,256]{3,2,1,0:T(8,128)}, f32[2,4,32,256]{3,2,1,0:T(8,128)S(1)}, u32[]{:S(2)}, u32[]{:S(2)}) collective-permute-start(f32[2,4,32,256]{3,2,1,0:T(8,128)} %copy.35), channel_id=1, source_target_pairs={{0,16},{1,17},{2,18},{3,19},{4,20},{5,21},{6,22},{7,23},{8,24},{9,... | collective-permute-start | bytes 786440 | tf_op jit(solution)/shard_map/ppermute | solution.py:14
  57.2 9.3 %collective-permute-start.1 = (f32[2,4,32,256]{3,2,1,0:T(8,128)}, f32[2,4,32,256]{3,2,1,0:T(8,128)}, u32[]{:S(2)}, u32[]{:S(2)}) collective-permute-start(f32[2,4,32,256]{3,2,1,0:T(8,128)} %copy.36), channel_id=1, source_target_pairs={{16,0},{17,1},{18,2},{19,3},{20,4},{21,5},{22,6},{23,7},{24,8},{25... | collective-permute-start | bytes 786440 | tf_op jit(solution)/shard_map/ppermute | solution.py:17
  82.1 20.1 %all-to-all-start.1 = ((f32[16,1,8192]{2,1,0:T(1,128)}), f32[16,1,8192]{2,1,0:T(1,128)}, u32[]{:S(2)}, u32[]{:S(2)}) async-start(f32[16,1,8192]{2,1,0:T(1,128)} %reshape.355), calls=%async_computation.1 | async-start | bytes 1048576 | tf_op jit(solution)/shard_map/all_to_all | solution.py:74
where the time goes:
time: 120 us; the launch traced here: 118 us
  local copies, waits for them, and re-layouts  36 us (30%)
  other arithmetic  32.1 us (27%)
  waiting for transfers between devices  25 us (21%)
  starting transfers between devices  17.7 us (15%)
  matrix products  7.21 us (6%)
    unnamed x30, local copies, waits for them, and re-layouts  13.1 us
    all_to_all x1, waiting for transfers between devices, per_device(): lax.all_to_all(spectrum, 'xline', split_axis=2, concat_axis=3, tiled=True)  12.9 us
    mul x1, other arithmetic, tables(): -weights[:, None] * sine.T  9.24 us
    neg x1, other arithmetic, tables(): forward_table = jnp.stack((cosine, -sine), axis=1)  8.24 us
    reduce_sum x3, other arithmetic, correlate(): jnp.sum(weight_real * piece_real - weight_imag * piece_imag, axis=0)  7.42 us
    all_to_all x1, starting transfers between devices, per_device(): lax.all_to_all(spectrum, 'xline', split_axis=2, concat_axis=3, tiled=True)  7.35 us
    all_to_all x2, local copies, waits for them, and re-layouts, per_device(): lax.all_to_all(result, 'xline', split_axis=3, concat_axis=2, tiled=True)  6.44 us
    ppermute x1, waiting for transfers between devices, extended(): lax.ppermute(lax.slice_in_dim(block, 0, width, axis=dim), axis, backward)  6.03 us
  transfers between devices with their start and end apart: 4, of which 4 were waited for; matrix products, arithmetic and copies ran while one was open for 11% of the time, Pallas kernels for 0%

commit v1 on v0

v1 whole, which is shorter than its diff:
```python
import functools

import jax
import jax.numpy as jnp
import ml_dtypes
import numpy as np
from jax import lax
from jax.experimental import pallas as pl
from jax.experimental.pallas import tpu as pltpu
from jax.sharding import PartitionSpec as P

HALF = 4
TAPS = 9
MESH = pl.DeviceIdType.MESH
BF16 = jnp.bfloat16
F32 = jnp.float32


def halves(table):
    high = table.astype(np.float32).astype(ml_dtypes.bfloat16)
    low = (table - high.astype(np.float64)).astype(np.float32).astype(ml_dtypes.bfloat16)
    return np.stack((high, low))


def temporal_tables(samples, frequencies):
    fold = samples // 2
    time = np.arange(fold)[:, None]
    forward, inverse = [], []
    for parity in range(2):
        bins = np.arange(parity, frequencies, 2)[None, :]
        angle = 2.0 * np.pi * (time * bins % samples) / samples
        weight = np.where(bins == 0, 1.0, 2.0) / samples
        forward.append(np.concatenate((np.cos(angle), -np.sin(angle)), axis=1))
        inverse.append(np.concatenate((weight * np.cos(angle), -weight * np.sin(angle)), axis=1).T)
    return halves(np.stack(forward)), halves(np.stack(inverse))


def spatial_frequencies(height, width):
    chosen = []
    for row in range(height):
        for col in range(width):
            mirror = ((height - row) % height, (width - col) % width)
            if (row, col) <= mirror:
                chosen.append((row, col, 1.0 if (row, col) == mirror else 2.0))
    return np.array(chosen)


def spatial_basis(waves, padded, height, width, positions):
    positions = np.asarray(positions)
    turns = np.outer(waves[:, 0], positions[:, 0]) / height + np.outer(waves[:, 1], positions[:, 1]) / width
    angle = 2.0 * np.pi * turns
    basis = np.zeros((2 * padded, len(positions)))
    basis[: len(waves)] = np.cos(angle)
    basis[padded : padded + len(waves)] = np.sin(angle)
    return basis


def grid(rows, cols):
    return [(row, col) for row in rows for col in cols]


def spatial_tables(rows, cols, inline_count):
    height, width = rows + 2 * HALF, cols + 2 * HALF
    waves = spatial_frequencies(height, width)
    padded = -(-len(waves) // 16) * 16
    basis = functools.partial(spatial_basis, waves, padded, height, width)
    low, high = range(-HALF, 0), range(cols, cols + HALF)
    own = grid(range(rows), range(cols))
    first = basis(own + grid(range(rows), low) + grid(range(rows), high))
    above, below = range(-HALF, 0), range(rows, rows + HALF)
    if inline_count == 2:
        variants = [[below], [above]]
    else:
        variants = [[above, below]]
    second = []
    for sides in variants:
        places = []
        for side in sides:
            places += grid(side, range(cols))
        for side in sides:
            places += grid(side, low) + grid(side, high)
        second.append(halves(basis(places)))
    taps = basis(grid(range(-HALF, HALF + 1), range(-HALF, HALF + 1)))
    count = np.zeros((2 * padded, 1))
    count[: len(waves), 0] = waves[:, 2] / (height * width)
    count[padded : padded + len(waves), 0] = -waves[:, 2] / (height * width)
    back = (count * basis(own)).T
    return halves(first), np.stack(second), halves(taps), halves(back)


def parts(value):
    high = value.astype(BF16)
    return high, (value - high.astype(F32)).astype(BF16)


def product(left, right, dims=(((1,), (0,)), ((), ()))):
    dot = functools.partial(lax.dot_general, dimension_numbers=dims, preferred_element_type=F32)
    return dot(left[0], right[0]) + (dot(left[0], right[1]) + dot(left[1], right[0]))


def kernel(
    rows, cols, inline_count, xline_count,
    traces, filters, forward, inverse, first, second, taps, back,
    out,
    place, spec_high, spec_low, edge, corner, kept, wave, response,
    taps_in, forward_in, inverse_in, first_in, second_in, tapm_in, back_in,
    local_sem, send_sem, recv_sem,
):
    sides = min(inline_count - 1, 2)
    own = rows * cols
    strip = rows * HALF
    band = HALF * cols
    spot = HALF * HALF
    samples = place.shape[1]
    fold = samples // 2
    quarter = fold // 2
    padded = wave.shape[0] // 2
    left_at, right_at = own, own + strip
    band_at = own + 2 * strip
    spot_at = band_at + sides * band
    total = spot_at + sides * 2 * spot

    me_i = lax.axis_index("inline")
    me_x = lax.axis_index("xline")

    loads = [
        pltpu.make_async_copy(traces, place.at[pl.ds(0, own)], local_sem.at[0]),
        pltpu.make_async_copy(forward, forward_in, local_sem.at[1]),
        pltpu.make_async_copy(filters, taps_in, local_sem.at[2]),
        pltpu.make_async_copy(taps, tapm_in, local_sem.at[3]),
        pltpu.make_async_copy(first, first_in, local_sem.at[4]),
        pltpu.make_async_copy(second.at[me_i if inline_count == 2 else 0], second_in, local_sem.at[5]),
        pltpu.make_async_copy(back, back_in, local_sem.at[6]),
        pltpu.make_async_copy(inverse, inverse_in, local_sem.at[7]),
    ]
    for load in loads:
        load.start()

    has_left, has_right = me_x > 0, me_x < xline_count - 1
    neighbours = [(has_left, {"xline": me_x - 1}), (has_right, {"xline": me_x + 1})]
    if inline_count == 2:
        bands = [(None, {"inline": 1 - me_i}, (1 - me_i) * ((rows - HALF) * cols), 0)]
    elif inline_count > 2:
        bands = [
            (me_i > 0, {"inline": me_i - 1}, 0, 1),
            (me_i < inline_count - 1, {"inline": me_i + 1}, (rows - HALF) * cols, 0),
        ]
    else:
        bands = []
    neighbours += [(exists, where) for exists, where, _, _ in bands]

    def when(condition, action):
        if condition is None:
            action()
        else:
            pl.when(condition)(action)

    barrier = pltpu.get_barrier_semaphore()
    for exists, where in neighbours:
        when(exists, lambda: pl.semaphore_signal(barrier, inc=1, device_id=where, device_id_type=MESH))
    peers = sum(1 if exists is None else exists.astype(jnp.int32) for exists, _ in neighbours)
    pl.semaphore_wait(barrier, peers)

    def remote(source, target_at, size, slot, where):
        return pltpu.make_async_remote_copy(
            src_ref=source,
            dst_ref=place.at[pl.ds(target_at, size)],
            send_sem=send_sem.at[slot],
            recv_sem=recv_sem.at[slot],
            device_id=where,
            device_id_type=MESH,
        )

    for exists, where, start, lands in bands:
        start = pl.multiple_of(start, 8)
        copy = remote(traces.at[pl.ds(start, band)], band_at + lands * band, band, 2 + lands, where)
        when(exists, copy.start)

    loads[0].wait()
    for row in range(rows):
        at = row * cols
        edge[0, row * HALF : (row + 1) * HALF, :] = place[at : at + HALF, :]
        edge[1, row * HALF : (row + 1) * HALF, :] = place[at + cols - HALF : at + cols, :]
    to_left = remote(edge.at[0], right_at, strip, 1, {"xline": me_x - 1})
    to_right = remote(edge.at[1], left_at, strip, 0, {"xline": me_x + 1})
    when(has_left, to_left.start)
    when(has_right, to_right.start)

    loads[2].wait()
    loads[3].wait()
    across = (((1,), (1,)), ((), ()))
    for parity in range(2):
        for part in range(2):
            lanes = slice((2 * parity + part) * quarter, (2 * parity + part + 1) * quarter)
            coefficients = taps_in[part, pl.ds(parity, quarter, stride=2), :]
            response[:, lanes] = product((tapm_in[0], tapm_in[1]), parts(coefficients), across)

    def spectra(start, size):
        block = place[start : start + size, :]
        folded = (block[:, :fold] + block[:, fold:], block[:, :fold] - block[:, fold:])
        for parity in range(2):
            lanes = slice(parity * fold, (parity + 1) * fold)
            spectrum = product(parts(folded[parity]), (forward_in[0, parity], forward_in[1, parity]))
            high, low = parts(spectrum)
            spec_high[start : start + size, lanes] = high
            spec_low[start : start + size, lanes] = low

    loads[1].wait()
    spectra(0, own)

    for exists, copy, at in ((has_left, to_right, left_at), (has_right, to_left, right_at)):
        when(exists, copy.wait_recv)

        def clear(at=at):
            place[at : at + strip, :] = jnp.zeros((strip, samples), F32)

        pl.when(jnp.logical_not(exists))(clear)
    spectra(own, 2 * strip)
    loads[4].wait()
    for parity in range(2):
        lanes = slice(parity * fold, (parity + 1) * fold)
        wave[:, lanes] = product(
            (first_in[0], first_in[1]), (spec_high[:band_at, lanes], spec_low[:band_at, lanes])
        )

    for lands in range(sides):
        at = band_at + lands * band
        if inline_count == 2:
            exists = None
        else:
            exists = (me_i > 0) if lands == 0 else (me_i < inline_count - 1)
        incoming = remote(traces.at[pl.ds(0, band)], at, band, 2 + lands, {"xline": me_x})
        spots = [spot_at + (2 * lands + side) * spot for side in range(2)]
        slots = [4 + 2 * lands + side for side in range(2)]
        go_right = remote(corner.at[lands, 1], spots[0], spot, slots[0], {"xline": me_x + 1})
        go_left = remote(corner.at[lands, 0], spots[1], spot, slots[1], {"xline": me_x - 1})

        def arrive():
            incoming.wait_recv()
            for row in range(HALF):
                here = at + row * cols
                corner[lands, 0, row * HALF : (row + 1) * HALF, :] = place[here : here + HALF, :]
                corner[lands, 1, row * HALF : (row + 1) * HALF, :] = place[here + cols - HALF : here + cols, :]
            pl.when(has_right)(go_right.start)
            pl.when(has_left)(go_left.start)

        def absent():
            place[at : at + band, :] = jnp.zeros((band, samples), F32)
            for side in range(2):
                place[spots[side] : spots[side] + spot, :] = jnp.zeros((spot, samples), F32)

        when(exists, arrive)
        if exists is not None:
            pl.when(jnp.logical_not(exists))(absent)
    if sides:
        spectra(band_at, sides * band)
    for lands in range(sides):
        if inline_count == 2:
            exists = None
        else:
            exists = (me_i > 0) if lands == 0 else (me_i < inline_count - 1)
        for side, has in ((0, has_left), (1, has_right)):
            at = spot_at + (2 * lands + side) * spot
            come = remote(corner.at[lands, side], at, spot, 4 + 2 * lands + side, {"xline": me_x})

            def clear(at=at):
                place[at : at + spot, :] = jnp.zeros((spot, samples), F32)

            def get():
                pl.when(has)(come.wait_recv)
                pl.when(jnp.logical_not(has))(clear)

            when(exists, get)
    if sides:
        spectra(spot_at, sides * 2 * spot)
        loads[5].wait()
        for parity in range(2):
            lanes = slice(parity * fold, (parity + 1) * fold)
            wave[:, lanes] += product(
                (second_in[0], second_in[1]), (spec_high[band_at:total, lanes], spec_low[band_at:total, lanes])
            )
    else:
        loads[5].wait()

    loads[6].wait()
    loads[7].wait()
    halfway = []
    for parity in range(2):
        real = slice(2 * parity * quarter, (2 * parity + 1) * quarter)
        imag = slice((2 * parity + 1) * quarter, (2 * parity + 2) * quarter)
        rc, rs = wave[:padded, real], wave[padded:, real]
        ic, js = wave[:padded, imag], wave[padded:, imag]
        frc, frs = response[:padded, real], response[padded:, real]
        fic, fis = response[:padded, imag], response[padded:, imag]
        outcome = {
            (0, 0): rc * frc + rs * frs - (ic * fic + js * fis),
            (1, 0): rc * frs - rs * frc - (ic * fis - js * fic),
            (0, 1): rc * fic + rs * fis + (ic * frc + js * frs),
            (1, 1): rc * fis - rs * fic + (ic * frs - js * frc),
        }
        for (which, part), value in outcome.items():
            high, low = parts(value)
            kept[0, which * padded : (which + 1) * padded, part * quarter : (part + 1) * quarter] = high
            kept[1, which * padded : (which + 1) * padded, part * quarter : (part + 1) * quarter] = low
        filtered = product((back_in[0], back_in[1]), (kept[0], kept[1]))
        halfway.append(product(parts(filtered), (inverse_in[0, parity], inverse_in[1, parity])))
    out[:, :fold] = halfway[0] + halfway[1]
    out[:, fold:] = halfway[0] - halfway[1]

    when(has_left, to_left.wait_send)
    when(has_right, to_right.wait_send)
    for exists, where, start, lands in bands:
        copy = remote(traces.at[pl.ds(pl.multiple_of(start, 8), band)], band_at + lands * band, band, 2 + lands, where)
        when(exists, copy.wait_send)
    for lands in range(sides):
        if inline_count == 2:
            exists = None
        else:
            exists = (me_i > 0) if lands == 0 else (me_i < inline_count - 1)
        spots = [spot_at + (2 * lands + side) * spot for side in range(2)]
        go_right = remote(corner.at[lands, 1], spots[0], spot, 4 + 2 * lands, {"xline": me_x + 1})
        go_left = remote(corner.at[lands, 0], spots[1], spot, 5 + 2 * lands, {"xline": me_x - 1})

        def sent():
            pl.when(has_right)(go_right.wait_send)
            pl.when(has_left)(go_left.wait_send)

        when(exists, sent)


def per_device(traces, filters, inline_count, xline_count):
    rows, cols, samples = traces.shape
    frequencies = filters.shape[1]
    forward, inverse = temporal_tables(samples, frequencies)
    first, second, taps, back = spatial_tables(rows, cols, inline_count)
    sides = min(inline_count - 1, 2)
    own = rows * cols
    total = own + 2 * rows * HALF + sides * (HALF * cols + 2 * HALF * HALF)
    waves = first.shape[1]
    operands = [traces.reshape(own, samples), filters] + [
        jnp.asarray(table) for table in (forward, inverse, first, second, taps, back)
    ]
    result = pl.pallas_call(
        functools.partial(kernel, rows, cols, inline_count, xline_count),
        out_shape=jax.ShapeDtypeStruct((own, samples), F32),
        in_specs=[pl.BlockSpec(memory_space=pl.ANY)] * len(operands),
        out_specs=pl.BlockSpec(memory_space=pltpu.VMEM),
        scratch_shapes=[
            pltpu.VMEM((total, samples), F32),
            pltpu.VMEM((total, samples), BF16),
            pltpu.VMEM((total, samples), BF16),
            pltpu.VMEM((2, rows * HALF, samples), F32),
            pltpu.VMEM((max(sides, 1), 2, HALF * HALF, samples), F32),
            pltpu.VMEM((2, waves, samples // 2), BF16),
            pltpu.VMEM((waves, samples), F32),
            pltpu.VMEM((waves, samples), F32),
            pltpu.VMEM(filters.shape, F32),
            pltpu.VMEM(forward.shape, BF16),
            pltpu.VMEM(inverse.shape, BF16),
            pltpu.VMEM(first.shape, BF16),
            pltpu.VMEM(second.shape[1:], BF16),
            pltpu.VMEM(taps.shape, BF16),
            pltpu.VMEM(back.shape, BF16),
            pltpu.SemaphoreType.DMA((8,)),
            pltpu.SemaphoreType.DMA((8,)),
            pltpu.SemaphoreType.DMA((8,)),
        ],
        compiler_params=pltpu.CompilerParams(
            collective_id=0, has_side_effects=True, vmem_limit_bytes=48 * 1024 * 1024
        ),
    )(*operands)
    return result.reshape(rows, cols, samples)


def solution(mesh):
    return jax.shard_map(
        functools.partial(
            per_device, inline_count=mesh.shape["inline"], xline_count=mesh.shape["xline"]
        ),
        mesh=mesh,
        in_specs=(P("inline", "xline", None), P()),
        out_specs=P("inline", "xline", None),
        check_vma=False,
    )
```

time: 120 us -> 26.8 us (0.22)
  other arithmetic: 32.1 us -> 0 us
  local copies, waits for them, and re-layouts: 36 us -> 8.5 us
  waiting for transfers between devices: 25 us -> 0 us
  Pallas kernels: 0 us -> 17.9 us
  starting transfers between devices: 17.7 us -> 0 us
  matrix products: 7.21 us -> 0 us
    pallas_call x0 -> x1, Pallas kernels: none -> 17.9 us  [per_device(): pl.pallas_call(functools.partial(kernel, rows, cols, inline_count, xline_...]
    all_to_all x2 -> x0, waiting for transfers between devices: 17.8 us -> none  [the longest x1 12.9 us: per_device(): lax.all_to_all(spectrum, 'xline', split_axis=2, concat_axis=3, tiled=True)]
    all_to_all x2 -> x0, starting transfers between devices: 13.3 us -> none  [the longest x1 7.35 us: per_device(): lax.all_to_all(spectrum, 'xline', split_axis=2, concat_axis=3, tiled=True)]
    all_to_all x5 -> x0, local copies, waits for them, and re-layouts: 10.4 us -> none  [the longest x2 6.44 us: per_device(): lax.all_to_all(result, 'xline', split_axis=3, concat_axis=2, tiled=True)]
    mul x1 -> x0, other arithmetic: 9.24 us -> none  [tables(): -weights[:, None] * sine.T]
    neg x2 -> x0, other arithmetic: 8.24 us -> none  [the longest x1 8.24 us: tables(): forward_table = jnp.stack((cosine, -sine), axis=1)]
    reduce_sum x3 -> x0, other arithmetic: 7.42 us -> none  [correlate(): jnp.sum(weight_real * piece_real - weight_imag * piece_imag, axis=0)]
    dot_general x2 -> x0, matrix products: 7.21 us -> none  [the longest x1 4.78 us: per_device(): jnp.einsum('pifx,pft->ixt', returned, inverse_table, precision=highest)]
  transfers between devices with their start and end apart: 4 -> 0, of which waited for: 4 -> 0; matrix products, arithmetic and copies ran while one was open for 11% -> 0% of each run, Pallas kernels for 0% -> 0%
where the time goes in v1:
time: 26.8 us; the launch traced here: 26.4 us
  Pallas kernels  17.9 us (67%)
  local copies, waits for them, and re-layouts  8.5 us (32%)
    pallas_call x1, Pallas kernels, per_device(): pl.pallas_call(functools.partial(kernel, rows, cols, inline_count, xline_...  17.9 us
    unnamed x14, local copies, waits for them, and re-layouts  8.5 us

profile of v1, /device:TPU:1, one launch (start us, length us, event | category | flops | bytes accessed | tf_op | source)
XLA Modules:
  0.0 26.4 jit_solution(10838298244776533914)
XLA Ops:
  0.0 1.2 %copy.9.filters = f32[2,512,81]{2,1,0:T(8,128)S(1)} copy(f32[2,512,81]{1,0,2:T(2,128)} %param.9) | data formatting | bytes 663552 | tf_op args[1]
  1.2 0.0 copy-start
  1.2 1.6 %copy-done = bf16[2,2,512,512]{3,2,1,0:T(8,128)(2,1)S(1)} copy-done((bf16[2,2,512,512]{3,2,1,0:T(8,128)(2,1)S(1)}, bf16[2,2,512,512]{3,2,1,0:T(8,128)(2,1)}, u32[]{:S(2)}) %copy-start) | copy-done | bytes 2097176
  2.8 0.0 copy-start.1
  2.8 1.0 %copy-done.1 = f32[8,16,1024]{2,1,0:T(8,128)S(1)} copy-done((f32[8,16,1024]{2,1,0:T(8,128)S(1)}, f32[8,16,1024]{2,1,0:T(8,128)}, u32[]{:S(2)}) %copy-start.1) | copy-done | bytes 524312
  3.8 0.0 copy-start.2
  3.8 1.0 %copy-done.2 = bf16[2,2,416,96]{3,2,1,0:T(8,128)(2,1)S(1)} copy-done((bf16[2,2,416,96]{3,2,1,0:T(8,128)(2,1)S(1)}, bf16[2,2,416,96]{3,2,1,0:T(8,128)(2,1)}, u32[]{:S(2)}) %copy-start.2) | copy-done | bytes 319512
  4.8 0.0 copy-start.3
  4.8 1.0 %copy-done.3 = bf16[2,416,192]{2,1,0:T(8,128)(2,1)S(1)} copy-done((bf16[2,416,192]{2,1,0:T(8,128)(2,1)S(1)}, bf16[2,416,192]{2,1,0:T(8,128)(2,1)}, u32[]{:S(2)}) %copy-start.3) | copy-done | bytes 319512
  5.8 0.0 copy-start.4
  5.8 0.9 %copy-done.4 = bf16[2,128,416]{2,1,0:T(8,128)(2,1)S(1)} copy-done((bf16[2,128,416]{2,1,0:T(8,128)(2,1)S(1)}, bf16[2,128,416]{2,1,0:T(8,128)(2,1)}, u32[]{:S(2)}) %copy-start.4) | copy-done | bytes 213016
  6.8 0.0 copy-start.5
  6.8 0.9 %copy-done.5 = bf16[2,416,81]{2,1,0:T(8,128)(2,1)S(1)} copy-done((bf16[2,416,81]{2,1,0:T(8,128)(2,1)S(1)}, bf16[2,416,81]{2,1,0:T(8,128)(2,1)}, u32[]{:S(2)}) %copy-start.5) | copy-done | bytes 134808
  7.7 17.9 %shard_map.82 = f32[128,1024]{1,0:T(8,128)S(1)} custom-call(f32[128,1024]{1,0:T(8,128)S(1)} %bitcast.3, f32[2,512,81]{2,1,0:T(8,128)S(1)} %copy.9.filters, bf16[2,2,512,512]{3,2,1,0:T(8,128)(2,1)S(1)} %copy-done, bf16[2,2,512,512]{3,2,1,0:T(8,128)(2,1)} %constant.13.clone.inverse, bf16[2,416,192]{2,1,0:T(8,128)(2,1)S(1)} %copy-done.3, ...), custom_call_target="tpu_custom_call" | custom-call | tf_op jit(solution)/shard_map/pallas_call | solution.py:343
  25.6 0.8 %copy.11 = f32[8,16,1024]{2,1,0:T(8,128)} copy(f32[8,16,1024]{2,1,0:T(8,128)S(1)} %bitcast.2) | data formatting | bytes 1048576
Async XLA Ops:
  1.2 1.6 %copy-start = (bf16[2,2,512,512]{3,2,1,0:T(8,128)(2,1)S(1)}, bf16[2,2,512,512]{3,2,1,0:T(8,128)(2,1)}, u32[]{:S(2)}) copy-start(bf16[2,2,512,512]{3,2,1,0:T(8,128)(2,1)} %constant.12.clone.forward) | copy-start | bytes 6291460
  2.8 1.0 %copy-start.1 = (f32[8,16,1024]{2,1,0:T(8,128)S(1)}, f32[8,16,1024]{2,1,0:T(8,128)}, u32[]{:S(2)}) copy-start(f32[8,16,1024]{2,1,0:T(8,128)} %param.8) | copy-start | bytes 1572868
  3.8 1.0 %copy-start.2 = (bf16[2,2,416,96]{3,2,1,0:T(8,128)(2,1)S(1)}, bf16[2,2,416,96]{3,2,1,0:T(8,128)(2,1)}, u32[]{:S(2)}) copy-start(bf16[2,2,416,96]{3,2,1,0:T(8,128)(2,1)} %constant.15.clone.second) | copy-start | bytes 958468
  4.8 1.0 %copy-start.3 = (bf16[2,416,192]{2,1,0:T(8,128)(2,1)S(1)}, bf16[2,416,192]{2,1,0:T(8,128)(2,1)}, u32[]{:S(2)}) copy-start(bf16[2,416,192]{2,1,0:T(8,128)(2,1)} %constant.14.clone.first) | copy-start | bytes 958468
  5.8 0.9 %copy-start.4 = (bf16[2,128,416]{2,1,0:T(8,128)(2,1)S(1)}, bf16[2,128,416]{2,1,0:T(8,128)(2,1)}, u32[]{:S(2)}) copy-start(bf16[2,128,416]{2,1,0:T(8,128)(2,1)} %constant.17.clone.back) | copy-start | bytes 638980
  6.8 0.9 %copy-start.5 = (bf16[2,416,81]{2,1,0:T(8,128)(2,1)S(1)}, bf16[2,416,81]{2,1,0:T(8,128)(2,1)}, u32[]{:S(2)}) copy-start(bf16[2,416,81]{2,1,0:T(8,128)(2,1)} %constant.16.clone.taps) | copy-start | bytes 404356

commit v2 on v0

v2 whole, which is shorter than its diff:
```python
import functools

import jax
import jax.numpy as jnp
import ml_dtypes
import numpy as np
from jax import lax
from jax.experimental import pallas as pl
from jax.experimental.pallas import tpu as pltpu
from jax.sharding import PartitionSpec as P

HALF = 4
GROUPS = 2
TAP_ROWS = 96
MESH = pl.DeviceIdType.MESH
BF16 = jnp.bfloat16
F32 = jnp.float32


def halves(table):
    high = table.astype(np.float32).astype(ml_dtypes.bfloat16)
    low = (table - high.astype(np.float64)).astype(np.float32).astype(ml_dtypes.bfloat16)
    return np.stack((high, low))


def bin_groups(frequencies):
    order = np.concatenate((np.arange(0, frequencies, 2), np.arange(1, frequencies, 2)))
    return order.reshape(GROUPS, frequencies // GROUPS)


def temporal_tables(samples, frequencies):
    time = np.arange(samples // 2)[:, None]
    forward, inverse = [], []
    for bins in bin_groups(frequencies):
        angle = 2.0 * np.pi * (time * bins[None, :] % samples) / samples
        weight = np.where(bins == 0, 1.0, 2.0)[None, :] / samples
        forward.append(np.concatenate((np.cos(angle), -np.sin(angle)), axis=1))
        inverse.append(np.concatenate((weight * np.cos(angle), -weight * np.sin(angle)), axis=1).T)
    return halves(np.stack(forward)), halves(np.stack(inverse))


def spatial_frequencies(height, width):
    chosen = []
    for row in range(height):
        for col in range(width):
            mirror = ((height - row) % height, (width - col) % width)
            if (row, col) <= mirror:
                chosen.append((row, col, 1.0 if (row, col) == mirror else 2.0))
    return np.array(chosen)


def spatial_basis(waves, padded, height, width, positions):
    positions = np.asarray(positions)
    turns = np.outer(waves[:, 0], positions[:, 0]) / height + np.outer(waves[:, 1], positions[:, 1]) / width
    angle = 2.0 * np.pi * turns
    basis = np.zeros((2 * padded, len(positions)))
    basis[: len(waves)] = np.cos(angle)
    basis[padded : padded + len(waves)] = np.sin(angle)
    return basis


def grid(rows, cols):
    return [(row, col) for row in rows for col in cols]


def stacked(table):
    both = halves(table)
    return np.concatenate((both[0], both[1]), axis=0)


def layout(rows, cols, sides):
    strip, ends, middle = rows * HALF, HALF * HALF, HALF * (cols - 2 * HALF)
    sizes = [("left", strip), ("right", strip)]
    for side in range(sides):
        sizes += [(("low", side), ends), (("high", side), ends), (("middle", side), middle)]
        sizes += [(("from_left", side), ends), (("from_right", side), ends)]
    places, at = {}, 0
    for name, size in sizes:
        places[name] = (at, size)
        at += size
    return places, at


def spatial_tables(rows, cols, inline_count):
    height, width = rows + 2 * HALF, cols + 2 * HALF
    waves = spatial_frequencies(height, width)
    padded = -(-len(waves) // 16) * 16
    basis = functools.partial(spatial_basis, waves, padded, height, width)
    below_zero, above_end = range(-HALF, 0), range(cols, cols + HALF)
    own = grid(range(rows), range(cols))
    above, below = range(-HALF, 0), range(rows, rows + HALF)
    variants = [[below], [above]] if inline_count == 2 else [[above, below]]
    sides = min(inline_count - 1, 2)
    second = []
    for bands in variants:
        places = grid(range(rows), below_zero) + grid(range(rows), above_end)
        for band in bands[:sides]:
            places += grid(band, range(HALF)) + grid(band, range(cols - HALF, cols))
            places += grid(band, range(HALF, cols - HALF))
            places += grid(band, below_zero) + grid(band, above_end)
        second.append(stacked(basis(places)))
    reach = range(-HALF, HALF + 1)
    taps = np.zeros((2 * padded, TAP_ROWS))
    taps[:, : len(reach) ** 2] = basis(grid(reach, reach))
    count = np.zeros((2 * padded, 1))
    count[: len(waves), 0] = waves[:, 2] / (height * width)
    count[padded : padded + len(waves), 0] = -waves[:, 2] / (height * width)
    back = (count * basis(own)).T
    return stacked(basis(own)), np.stack(second), stacked(taps), stacked(back)


def parts(value):
    high = value.astype(BF16)
    return high, (value - high.astype(F32)).astype(BF16)


def product(left, high, low):
    dot = functools.partial(jnp.dot, preferred_element_type=F32)
    count = left.shape[0] // 2
    both = dot(left, high)
    return both[:count] + (both[count:] + dot(left[:count], low))


def kernel(
    rows, cols, inline_count, xline_count,
    traces, filters, forward, inverse, first, second, taps, back, order,
    out,
    own_in, own, own_high, own_low, ends, middle, halo, wave, response, kept, tap_rows,
    filters_in, forward_in, inverse_in, first_in, second_in, taps_in, back_in, order_in,
    local_sem, send_sem, recv_sem,
):
    sides = min(inline_count - 1, 2)
    places, _ = layout(rows, cols, sides)
    fold = own_in.shape[1] // 2
    lanes = wave.shape[2]
    bins = lanes // 2
    padded = wave.shape[1] // 2
    inner = cols - 2 * HALF

    me_i = lax.axis_index("inline")
    me_x = lax.axis_index("xline")

    def load(source, target, slot):
        return pltpu.make_async_copy(source, target, local_sem.at[slot])

    load_own = load(traces, own_in, 0)
    load_forward = [load(forward.at[:, group], forward_in.at[:, group], 1 + group) for group in range(GROUPS)]
    base = 1 + GROUPS
    load_filters = load(filters, filters_in, base)
    load_order = load(order, order_in, base + 1)
    load_taps = load(taps, taps_in, base + 2)
    load_first = load(first, first_in, base + 3)
    load_second = load(second.at[me_i if inline_count == 2 else 0], second_in, base + 4)
    load_back = load(back, back_in, base + 5)
    load_inverse = load(inverse, inverse_in, base + 6)
    loads = [load_own, *load_forward, load_filters, load_order, load_taps]
    loads += [load_first, load_second, load_back, load_inverse]
    for each in loads:
        each.start()

    has_left, has_right = me_x > 0, me_x < xline_count - 1
    at_left, at_right = {"xline": me_x - 1}, {"xline": me_x + 1}
    if inline_count == 2:
        bands = [(None, {"inline": 1 - me_i}, (1 - me_i) * (rows - HALF), 0)]
        present = [None]
    elif inline_count > 2:
        has_above, has_below = me_i > 0, me_i < inline_count - 1
        bands = [
            (has_above, {"inline": me_i - 1}, 0, 1),
            (has_below, {"inline": me_i + 1}, rows - HALF, 0),
        ]
        present = [has_above, has_below]
    else:
        bands, present = [], []

    def when(condition, action):
        if condition is None:
            action()
        else:
            pl.when(condition)(action)

    barrier = pltpu.get_barrier_semaphore()
    neighbours = [(has_left, at_left), (has_right, at_right)]
    neighbours += [(exists, where) for exists, where, _, _ in bands]
    for exists, where in neighbours:
        when(exists, lambda: pl.semaphore_signal(barrier, inc=1, device_id=where, device_id_type=MESH))

    def clear(*names):
        for name in names:
            at, size = places[name]
            halo[:, at : at + size, :] = jnp.zeros((GROUPS, size, lanes), F32)

    pl.when(jnp.logical_not(has_left))(lambda: clear("left", *[("from_left", s) for s in range(sides)]))
    pl.when(jnp.logical_not(has_right))(lambda: clear("right", *[("from_right", s) for s in range(sides)]))
    for side, exists in enumerate(present):
        if exists is not None:
            pieces = [(kind, side) for kind in ("low", "high", "middle", "from_left", "from_right")]
            pl.when(jnp.logical_not(exists))(lambda: clear(*pieces))

    slots = {name: slot for slot, name in enumerate(places)}

    def remote(group, name, source, where):
        at, size = places[name]
        slot = group * len(places) + slots[name]
        return pltpu.make_async_remote_copy(
            src_ref=source,
            dst_ref=halo.at[group, pl.ds(at, size)],
            send_sem=send_sem.at[slot],
            recv_sem=recv_sem.at[slot],
            device_id=where,
            device_id_type=MESH,
        )

    def landed(group, name):
        at, size = places[name]
        return halo.at[group, pl.ds(at, size)]

    def come(group, name):
        remote(group, name, landed(group, name), at_left).wait_recv()

    sent = []

    def send(condition, copy):
        when(condition, copy.start)
        sent.append((condition, copy))

    load_own.wait()
    for group in range(GROUPS):
        if group % (GROUPS // 2) == 0:
            if group == 0:
                folded = own_in[:, :fold] + own_in[:, fold:]
            else:
                folded = own_in[:, :fold] - own_in[:, fold:]
            folded = jnp.concatenate(parts(folded), axis=0)
        load_forward[group].wait()
        spectrum = product(folded, forward_in[0, group], forward_in[1, group])
        own[...] = spectrum
        high, low = parts(spectrum)
        own_high[group] = high
        own_low[group] = low
        for row in range(rows):
            at = row * cols
            ends[group, 0, row * HALF : (row + 1) * HALF, :] = own[at : at + HALF, :]
            ends[group, 1, row * HALF : (row + 1) * HALF, :] = own[at + cols - HALF : at + cols, :]
            middle[group, row * inner : (row + 1) * inner, :] = own[at + HALF : at + cols - HALF, :]
        if group == 0:
            peers = sum(1 if exists is None else exists.astype(jnp.int32) for exists, _ in neighbours)
            pl.semaphore_wait(barrier, peers)
        for exists, where, start, side in bands:
            few = pl.ds(pl.multiple_of(start * HALF, HALF * HALF), HALF * HALF)
            many = pl.ds(pl.multiple_of(start * inner, HALF * inner), HALF * inner)
            send(exists, remote(group, ("low", side), ends.at[group, 0, few], where))
            send(exists, remote(group, ("high", side), ends.at[group, 1, few], where))
            send(exists, remote(group, ("middle", side), middle.at[group, many], where))
        send(has_left, remote(group, "right", ends.at[group, 0], at_left))
        send(has_right, remote(group, "left", ends.at[group, 1], at_right))

    def forward_ends(group):
        for side, exists in enumerate(present):
            def on(side=side):
                come(group, ("low", side))
                come(group, ("high", side))
                to_left = remote(group, ("from_right", side), landed(group, ("low", side)), at_left)
                to_right = remote(group, ("from_left", side), landed(group, ("high", side)), at_right)
                pl.when(has_left)(to_left.start)
                pl.when(has_right)(to_right.start)

            when(exists, on)

    def sent_ends(group):
        for side, exists in enumerate(present):
            def on(side=side):
                to_left = remote(group, ("from_right", side), landed(group, ("low", side)), at_left)
                to_right = remote(group, ("from_left", side), landed(group, ("high", side)), at_right)
                pl.when(has_left)(to_left.wait_send)
                pl.when(has_right)(to_right.wait_send)

            when(exists, on)

    load_filters.wait()
    load_order.wait()
    load_taps.wait()
    tap_count = filters_in.shape[0]
    tap_rows[...] = jnp.zeros_like(tap_rows)
    for part in range(2):
        tap_rows[part, :tap_count, :] = filters_in[:, part, :]
    real, imag = parts(tap_rows[0]), parts(tap_rows[1])
    ordered = jnp.dot(
        jnp.concatenate((real[0], imag[0], real[1], imag[1]), axis=0), order_in[...], preferred_element_type=F32
    ).astype(BF16)
    for group in range(GROUPS):
        mine = slice(group * bins, (group + 1) * bins)
        pieces = [ordered[TAP_ROWS * piece : TAP_ROWS * (piece + 1), mine] for piece in range(4)]
        response[group] = product(
            taps_in[...], jnp.concatenate(pieces[:2], axis=1), jnp.concatenate(pieces[2:], axis=1)
        )
    load_first.wait()
    for group in range(GROUPS):
        wave[group] = product(first_in[...], own_high[group], own_low[group])

    load_second.wait()
    load_back.wait()
    load_inverse.wait()
    forward_ends(0)
    halfway = [None, None]
    for group in range(GROUPS):
        pl.when(has_left)(lambda: come(group, "left"))
        pl.when(has_right)(lambda: come(group, "right"))
        for side, exists in enumerate(present):
            def rest(side=side):
                come(group, ("middle", side))
                pl.when(has_left)(lambda: come(group, ("from_left", side)))
                pl.when(has_right)(lambda: come(group, ("from_right", side)))

            when(exists, rest)
        high, low = parts(halo[group])
        wave[group] += product(second_in[...], high, low)
        if group + 1 < GROUPS:
            forward_ends(group + 1)

        rc, rs = wave[group, :padded, :bins], wave[group, padded:, :bins]
        ic, js = wave[group, :padded, bins:], wave[group, padded:, bins:]
        frc, frs = response[group, :padded, :bins], response[group, padded:, :bins]
        fic, fis = response[group, :padded, bins:], response[group, padded:, bins:]
        outcome = {
            (0, 0): rc * frc + rs * frs - (ic * fic + js * fis),
            (1, 0): rc * frs - rs * frc - (ic * fis - js * fic),
            (0, 1): rc * fic + rs * fis + (ic * frc + js * frs),
            (1, 1): rc * fis - rs * fic + (ic * frs - js * frc),
        }
        for (which, part), value in outcome.items():
            high, low = parts(value)
            kept[0, which * padded : (which + 1) * padded, part * bins : (part + 1) * bins] = high
            kept[1, which * padded : (which + 1) * padded, part * bins : (part + 1) * bins] = low
        filtered = product(back_in[...], kept[0], kept[1])
        filtered = jnp.concatenate(parts(filtered), axis=0)
        piece = product(filtered, inverse_in[0, group], inverse_in[1, group])
        parity = group // (GROUPS // 2)
        halfway[parity] = piece if halfway[parity] is None else halfway[parity] + piece
    out[:, :fold] = halfway[0] + halfway[1]
    out[:, fold:] = halfway[0] - halfway[1]

    for condition, copy in sent:
        when(condition, copy.wait_send)
    for group in range(GROUPS):
        sent_ends(group)


def per_device(traces, filters, inline_count, xline_count):
    rows, cols, samples = traces.shape
    _, frequencies, tap_count = filters.shape
    forward, inverse = temporal_tables(samples, frequencies)
    first, second, taps, back = spatial_tables(rows, cols, inline_count)
    order = np.zeros((frequencies, frequencies), ml_dtypes.bfloat16)
    order[bin_groups(frequencies).reshape(-1), np.arange(frequencies)] = 1.0
    sides = min(inline_count - 1, 2)
    places, around = layout(rows, cols, sides)
    own = rows * cols
    waves = first.shape[0] // 2
    lanes = 2 * frequencies // GROUPS
    tables = (forward, inverse, first, second, taps, back, order)
    operands = [traces.reshape(own, samples), filters.transpose(2, 0, 1)]
    operands += [jnp.asarray(table) for table in tables]
    copies = GROUPS * len(places)
    result = pl.pallas_call(
        functools.partial(kernel, rows, cols, inline_count, xline_count),
        out_shape=jax.ShapeDtypeStruct((own, samples), F32),
        in_specs=[pl.BlockSpec(memory_space=pltpu.HBM)] * len(operands),
        out_specs=pl.BlockSpec(memory_space=pltpu.VMEM),
        scratch_shapes=[
            pltpu.VMEM((own, samples), F32),
            pltpu.VMEM((own, lanes), F32),
            pltpu.VMEM((GROUPS, own, lanes), BF16),
            pltpu.VMEM((GROUPS, own, lanes), BF16),
            pltpu.VMEM((GROUPS, 2, rows * HALF, lanes), F32),
            pltpu.VMEM((GROUPS, rows * (cols - 2 * HALF), lanes), F32),
            pltpu.VMEM((GROUPS, around, lanes), F32),
            pltpu.VMEM((GROUPS, waves, lanes), F32),
            pltpu.VMEM((GROUPS, waves, lanes), F32),
            pltpu.VMEM((2, waves, lanes), BF16),
            pltpu.VMEM((2, TAP_ROWS, frequencies), F32),
            pltpu.VMEM((tap_count, 2, frequencies), F32),
            pltpu.VMEM(forward.shape, BF16),
            pltpu.VMEM(inverse.shape, BF16),
            pltpu.VMEM(first.shape, BF16),
            pltpu.VMEM(second.shape[1:], BF16),
            pltpu.VMEM(taps.shape, BF16),
            pltpu.VMEM(back.shape, BF16),
            pltpu.VMEM(order.shape, BF16),
            pltpu.SemaphoreType.DMA((8 + GROUPS,)),
            pltpu.SemaphoreType.DMA((copies,)),
            pltpu.SemaphoreType.DMA((copies,)),
        ],
        compiler_params=pltpu.CompilerParams(
            collective_id=0, has_side_effects=True, vmem_limit_bytes=48 * 1024 * 1024
        ),
    )(*operands)
    return result.reshape(rows, cols, samples)


def solution(mesh):
    return jax.shard_map(
        functools.partial(
            per_device, inline_count=mesh.shape["inline"], xline_count=mesh.shape["xline"]
        ),
        mesh=mesh,
        in_specs=(P("inline", "xline", None), P()),
        out_specs=P("inline", "xline", None),
        check_vma=False,
    )
```

time: 120 us -> 24.5 us (0.20)
  other arithmetic: 32.1 us -> 0 us
  local copies, waits for them, and re-layouts: 36 us -> 9.41 us
  waiting for transfers between devices: 25 us -> 0 us
  starting transfers between devices: 17.7 us -> 0 us
  Pallas kernels: 0 us -> 14.6 us
  matrix products: 7.21 us -> 0 us
    all_to_all x2 -> x0, waiting for transfers between devices: 17.8 us -> none  [the longest x1 12.9 us: per_device(): lax.all_to_all(spectrum, 'xline', split_axis=2, concat_axis=3, tiled=True)]
    pallas_call x0 -> x1, Pallas kernels: none -> 14.6 us  [per_device(): pl.pallas_call(functools.partial(kernel, rows, cols, inline_count, xline_...]
    all_to_all x2 -> x0, starting transfers between devices: 13.3 us -> none  [the longest x1 7.35 us: per_device(): lax.all_to_all(spectrum, 'xline', split_axis=2, concat_axis=3, tiled=True)]
    all_to_all x5 -> x0, local copies, waits for them, and re-layouts: 10.4 us -> none  [the longest x2 6.44 us: per_device(): lax.all_to_all(result, 'xline', split_axis=3, concat_axis=2, tiled=True)]
    mul x1 -> x0, other arithmetic: 9.24 us -> none  [tables(): -weights[:, None] * sine.T]
    neg x2 -> x0, other arithmetic: 8.24 us -> none  [the longest x1 8.24 us: tables(): forward_table = jnp.stack((cosine, -sine), axis=1)]
    reduce_sum x3 -> x0, other arithmetic: 7.42 us -> none  [correlate(): jnp.sum(weight_real * piece_real - weight_imag * piece_imag, axis=0)]
    dot_general x2 -> x0, matrix products: 7.21 us -> none  [the longest x1 4.78 us: per_device(): jnp.einsum('pifx,pft->ixt', returned, inverse_table, precision=highest)]
  transfers between devices with their start and end apart: 4 -> 0, of which waited for: 4 -> 0; matrix products, arithmetic and copies ran while one was open for 11% -> 0% of each run, Pallas kernels for 0% -> 0%
where the time goes in v2:
time: 24.5 us; the launch traced here: 24.1 us
  Pallas kernels  14.6 us (60%)
  local copies, waits for them, and re-layouts  9.41 us (38%)
    pallas_call x1, Pallas kernels, per_device(): pl.pallas_call(functools.partial(kernel, rows, cols, inline_count, xline_...  14.6 us
    unnamed x17, local copies, waits for them, and re-layouts  9.41 us

profile of v2, /device:TPU:1, one launch (start us, length us, event | category | flops | bytes accessed | tf_op | source)
XLA Modules:
  0.0 24.1 jit_solution(14309161202009217478)
XLA Ops:
  0.0 0.0 copy-start
  0.0 1.6 %copy-done = bf16[2,2,512,512]{3,2,1,0:T(8,128)(2,1)S(1)} copy-done((bf16[2,2,512,512]{3,2,1,0:T(8,128)(2,1)S(1)}, bf16[2,2,512,512]{3,2,1,0:T(8,128)(2,1)}, u32[]{:S(2)}) %copy-start) | copy-done | bytes 2097176
  1.6 0.0 copy-start.1
  1.6 1.2 %copy-done.1 = bf16[2,832,160]{2,1,0:T(8,128)(2,1)S(1)} copy-done((bf16[2,832,160]{2,1,0:T(8,128)(2,1)S(1)}, bf16[2,832,160]{2,1,0:T(8,128)(2,1)}, u32[]{:S(2)}) %copy-start.1) | copy-done | bytes 532504
  2.7 0.0 copy-start.2
  2.8 1.0 %copy-done.2 = f32[8,16,1024]{2,1,0:T(8,128)S(1)} copy-done((f32[8,16,1024]{2,1,0:T(8,128)S(1)}, f32[8,16,1024]{2,1,0:T(8,128)}, u32[]{:S(2)}) %copy-start.2) | copy-done | bytes 524312
  3.8 0.0 copy-start.3
  3.8 1.0 %copy-done.3 = bf16[512,512]{1,0:T(8,128)(2,1)S(1)} copy-done((bf16[512,512]{1,0:T(8,128)(2,1)S(1)}, bf16[512,512]{1,0:T(8,128)(2,1)}, u32[]{:S(2)}) %copy-start.3) | copy-done | bytes 524312
  4.8 0.0 copy-start.4
  4.8 1.0 %copy-done.4 = f32[2,512,81]{1,0,2:T(2,128)S(1)} copy-done((f32[2,512,81]{1,0,2:T(2,128)S(1)}, f32[2,512,81]{1,0,2:T(2,128)}, u32[]{:S(2)}) %copy-start.4) | copy-done | bytes 331800
  5.8 0.0 copy-start.5
  5.8 0.9 %copy-done.5 = bf16[256,416]{1,0:T(8,128)(2,1)S(1)} copy-done((bf16[256,416]{1,0:T(8,128)(2,1)S(1)}, bf16[256,416]{1,0:T(8,128)(2,1)}, u32[]{:S(2)}) %copy-start.5) | copy-done | bytes 213016
  6.8 0.0 copy-start.6
  6.8 0.9 %copy-done.6 = bf16[832,96]{1,0:T(8,128)(2,1)S(1)} copy-done((bf16[832,96]{1,0:T(8,128)(2,1)S(1)}, bf16[832,96]{1,0:T(8,128)(2,1)}, u32[]{:S(2)}) %copy-start.6) | copy-done | bytes 159768
  7.7 0.0 copy-start.7
  7.7 0.9 %copy-done.7 = bf16[832,128]{1,0:T(8,128)(2,1)S(1)} copy-done((bf16[832,128]{1,0:T(8,128)(2,1)S(1)}, bf16[832,128]{1,0:T(8,128)(2,1)}, u32[]{:S(2)}) %copy-start.7) | copy-done | bytes 213016
  8.6 14.6 %shard_map.91 = f32[128,1024]{1,0:T(8,128)S(1)} custom-call(f32[128,1024]{1,0:T(8,128)S(1)} %bitcast.4, f32[81,2,512]{2,1,0:T(2,128)S(1)} %bitcast.5, bf16[2,2,512,512]{3,2,1,0:T(8,128)(2,1)S(1)} %copy-done, bf16[2,2,512,512]{3,2,1,0:T(8,128)(2,1)} %constant.15.clone.inverse, bf16[832,128]{1,0:T(8,128)(2,1)S(1)} %copy-done.7, ...), custom_call_target="tpu_custom_call" | custom-call | tf_op jit(solution)/shard_map/pallas_call | solution.py:365
  23.3 0.8 %copy.11 = f32[8,16,1024]{2,1,0:T(8,128)} copy(f32[8,16,1024]{2,1,0:T(8,128)S(1)} %bitcast.3) | data formatting | bytes 1048576
Async XLA Ops:
  0.0 1.6 %copy-start = (bf16[2,2,512,512]{3,2,1,0:T(8,128)(2,1)S(1)}, bf16[2,2,512,512]{3,2,1,0:T(8,128)(2,1)}, u32[]{:S(2)}) copy-start(bf16[2,2,512,512]{3,2,1,0:T(8,128)(2,1)} %constant.14.clone.forward) | copy-start | bytes 6291460
  1.6 1.2 %copy-start.1 = (bf16[2,832,160]{2,1,0:T(8,128)(2,1)S(1)}, bf16[2,832,160]{2,1,0:T(8,128)(2,1)}, u32[]{:S(2)}) copy-start(bf16[2,832,160]{2,1,0:T(8,128)(2,1)} %constant.17.clone.second) | copy-start | bytes 1597444
  2.7 1.0 %copy-start.2 = (f32[8,16,1024]{2,1,0:T(8,128)S(1)}, f32[8,16,1024]{2,1,0:T(8,128)}, u32[]{:S(2)}) copy-start(f32[8,16,1024]{2,1,0:T(8,128)} %param.9) | copy-start | bytes 1572868
  3.8 1.0 %copy-start.3 = (bf16[512,512]{1,0:T(8,128)(2,1)S(1)}, bf16[512,512]{1,0:T(8,128)(2,1)}, u32[]{:S(2)}) copy-start(bf16[512,512]{1,0:T(8,128)(2,1)} %constant.20.clone.order) | copy-start | bytes 1572868
  4.8 1.0 %copy-start.4 = (f32[2,512,81]{1,0,2:T(2,128)S(1)}, f32[2,512,81]{1,0,2:T(2,128)}, u32[]{:S(2)}) copy-start(f32[2,512,81]{1,0,2:T(2,128)} %param.10) | copy-start | bytes 995332
  5.8 0.9 %copy-start.5 = (bf16[256,416]{1,0:T(8,128)(2,1)S(1)}, bf16[256,416]{1,0:T(8,128)(2,1)}, u32[]{:S(2)}) copy-start(bf16[256,416]{1,0:T(8,128)(2,1)} %constant.19.clone.back) | copy-start | bytes 638980
  6.8 0.9 %copy-start.6 = (bf16[832,96]{1,0:T(8,128)(2,1)S(1)}, bf16[832,96]{1,0:T(8,128)(2,1)}, u32[]{:S(2)}) copy-start(bf16[832,96]{1,0:T(8,128)(2,1)} %constant.18.clone.taps) | copy-start | bytes 479236
  7.7 0.9 %copy-start.7 = (bf16[832,128]{1,0:T(8,128)(2,1)S(1)}, bf16[832,128]{1,0:T(8,128)(2,1)}, u32[]{:S(2)}) copy-start(bf16[832,128]{1,0:T(8,128)(2,1)} %constant.16.clone.first) | copy-start | bytes 638980

commit v3 on v2

--- a/solution.py
+++ b/solution.py
@@ -392,7 +392,7 @@
             pltpu.SemaphoreType.DMA((copies,)),
         ],
         compiler_params=pltpu.CompilerParams(
-            collective_id=0, has_side_effects=True, vmem_limit_bytes=48 * 1024 * 1024
+            collective_id=0, has_side_effects=True, vmem_limit_bytes=60 * 1024 * 1024
         ),
     )(*operands)
     return result.reshape(rows, cols, samples)

time: 24.5 us -> 17.6 us (0.72); the launches traced: 24.1 us -> 17.5 us
  local copies, waits for them, and re-layouts: 9.41 us -> 1.89 us
  Pallas kernels: 14.6 us -> 15.6 us
    unnamed x17 -> x1, local copies, waits for them, and re-layouts: 9.41 us -> 1.89 us
    pallas_call x1, Pallas kernels: 14.6 us -> 15.6 us  [per_device(): pl.pallas_call(functools.partial(kernel, rows, cols, inline_count, xline_...]
where the time goes in v3:
time: 17.6 us; the launch traced here: 17.5 us
  Pallas kernels  15.6 us (89%)
  local copies, waits for them, and re-layouts  1.89 us (11%)
    pallas_call x1, Pallas kernels, per_device(): pl.pallas_call(functools.partial(kernel, rows, cols, inline_count, xline_...  15.6 us
    unnamed x1, local copies, waits for them, and re-layouts  1.89 us

profile of v3, /device:TPU:1, one launch (start us, length us, event | category | flops | bytes accessed | tf_op | source)
XLA Modules:
  0.0 17.5 jit_solution(5044379449961970693)
XLA Ops:
  0.0 15.6 %shard_map.91 = f32[128,1024]{1,0:T(8,128)} custom-call(f32[128,1024]{1,0:T(8,128)} %bitcast.4, f32[81,2,512]{2,1,0:T(2,128)} %bitcast.5, bf16[2,2,512,512]{3,2,1,0:T(8,128)(2,1)} %constant.14.clone.forward, bf16[2,2,512,512]{3,2,1,0:T(8,128)(2,1)} %constant.15.clone.inverse, bf16[832,128]{1,0:T(8,128)(2,1)} %constant.16.clone.first, ...), custom_call_target="tpu_custom_call" | custom-call | tf_op jit(solution)/shard_map/pallas_call | solution.py:365
  15.6 1.9 %copy.11 = f32[8,16,1024]{2,1,0:T(8,128)} copy(f32[8,16,1024]{2,1,0:T(8,128)} %bitcast.3) | data formatting | bytes 1048576

commit v4 on v3

--- a/solution.py
+++ b/solution.py
@@ -248,12 +248,14 @@
             pl.semaphore_wait(barrier, peers)
         for exists, where, start, side in bands:
             few = pl.ds(pl.multiple_of(start * HALF, HALF * HALF), HALF * HALF)
-            many = pl.ds(pl.multiple_of(start * inner, HALF * inner), HALF * inner)
             send(exists, remote(group, ("low", side), ends.at[group, 0, few], where))
             send(exists, remote(group, ("high", side), ends.at[group, 1, few], where))
-            send(exists, remote(group, ("middle", side), middle.at[group, many], where))
         send(has_left, remote(group, "right", ends.at[group, 0], at_left))
         send(has_right, remote(group, "left", ends.at[group, 1], at_right))
+    for group in range(GROUPS):
+        for exists, where, start, side in bands:
+            many = pl.ds(pl.multiple_of(start * inner, HALF * inner), HALF * inner)
+            send(exists, remote(group, ("middle", side), middle.at[group, many], where))
 
     def forward_ends(group):
         for side, exists in enumerate(present):
@@ -294,14 +296,17 @@
         response[group] = product(
             taps_in[...], jnp.concatenate(pieces[:2], axis=1), jnp.concatenate(pieces[2:], axis=1)
         )
+        if group < GROUPS - 1:
+            forward_ends(group)
     load_first.wait()
     for group in range(GROUPS):
         wave[group] = product(first_in[...], own_high[group], own_low[group])
+        if group == 0:
+            forward_ends(GROUPS - 1)
 
     load_second.wait()
     load_back.wait()
     load_inverse.wait()
-    forward_ends(0)
     halfway = [None, None]
     for group in range(GROUPS):
         pl.when(has_left)(lambda: come(group, "left"))
@@ -315,8 +320,6 @@
             when(exists, rest)
         high, low = parts(halo[group])
         wave[group] += product(second_in[...], high, low)
-        if group + 1 < GROUPS:
-            forward_ends(group + 1)
 
         rc, rs = wave[group, :padded, :bins], wave[group, padded:, :bins]
         ic, js = wave[group, :padded, bins:], wave[group, padded:, bins:]

time: 17.6 us -> 16.6 us (0.943)
  Pallas kernels: 15.6 us -> 14.5 us
    pallas_call x1, Pallas kernels: 15.6 us -> 14.5 us  [per_device(): pl.pallas_call(functools.partial(kernel, rows, cols, inline_count, xline_...]
where the time goes in v4:
time: 16.6 us; the launch traced here: 16.4 us
  Pallas kernels  14.5 us (87%)
  local copies, waits for them, and re-layouts  1.89 us (11%)
    pallas_call x1, Pallas kernels, per_device(): pl.pallas_call(functools.partial(kernel, rows, cols, inline_count, xline_...  14.5 us
    unnamed x1, local copies, waits for them, and re-layouts  1.89 us

profile of v4, /device:TPU:1, one launch (start us, length us, event | category | flops | bytes accessed | tf_op | source)
XLA Modules:
  0.0 16.4 jit_solution(12699295565286192166)
XLA Ops:
  0.0 14.5 %shard_map.91 = f32[128,1024]{1,0:T(8,128)} custom-call(f32[128,1024]{1,0:T(8,128)} %bitcast.4, f32[81,2,512]{2,1,0:T(2,128)} %bitcast.5, bf16[2,2,512,512]{3,2,1,0:T(8,128)(2,1)} %constant.14.clone.forward, bf16[2,2,512,512]{3,2,1,0:T(8,128)(2,1)} %constant.15.clone.inverse, bf16[832,128]{1,0:T(8,128)(2,1)} %constant.16.clone.first, ...), custom_call_target="tpu_custom_call" | custom-call | tf_op jit(solution)/shard_map/pallas_call | solution.py:368
  14.5 1.9 %copy.11 = f32[8,16,1024]{2,1,0:T(8,128)} copy(f32[8,16,1024]{2,1,0:T(8,128)} %bitcast.3) | data formatting | bytes 1048576

commit v5 on v4

--- a/solution.py
+++ b/solution.py
@@ -66,6 +66,11 @@
 def stacked(table):
     both = halves(table)
     return np.concatenate((both[0], both[1]), axis=0)
+
+
+def thrice(table):
+    both = halves(table)
+    return np.concatenate((both[0], both[0], both[1]), axis=1)
 
 
 def layout(rows, cols, sides):
@@ -98,7 +103,7 @@
             places += grid(band, range(HALF)) + grid(band, range(cols - HALF, cols))
             places += grid(band, range(HALF, cols - HALF))
             places += grid(band, below_zero) + grid(band, above_end)
-        second.append(stacked(basis(places)))
+        second.append(thrice(basis(places)))
     reach = range(-HALF, HALF + 1)
     taps = np.zeros((2 * padded, TAP_ROWS))
     taps[:, : len(reach) ** 2] = basis(grid(reach, reach))
@@ -106,7 +111,7 @@
     count[: len(waves), 0] = waves[:, 2] / (height * width)
     count[padded : padded + len(waves), 0] = -waves[:, 2] / (height * width)
     back = (count * basis(own)).T
-    return stacked(basis(own)), np.stack(second), stacked(taps), stacked(back)
+    return thrice(basis(own)), np.stack(second), thrice(taps), stacked(back)
 
 
 def parts(value):
@@ -119,6 +124,10 @@
     count = left.shape[0] // 2
     both = dot(left, high)
     return both[:count] + (both[count:] + dot(left[:count], low))
+
+
+def summed(left, high, low):
+    return jnp.dot(left, jnp.concatenate((high, low, high), axis=0), preferred_element_type=F32)
 
 
 def kernel(
@@ -140,6 +149,33 @@
     me_i = lax.axis_index("inline")
     me_x = lax.axis_index("xline")
 
+    has_left, has_right = me_x > 0, me_x < xline_count - 1
+    at_left, at_right = {"xline": me_x - 1}, {"xline": me_x + 1}
+    if inline_count == 2:
+        bands = [(None, {"inline": 1 - me_i}, (1 - me_i) * (rows - HALF), 0)]
+        present = [None]
+    elif inline_count > 2:
+        has_above, has_below = me_i > 0, me_i < inline_count - 1
+        bands = [
+            (has_above, {"inline": me_i - 1}, 0, 1),
+            (has_below, {"inline": me_i + 1}, rows - HALF, 0),
+        ]
+        present = [has_above, has_below]
+    else:
+        bands, present = [], []
+
+    def when(condition, action):
+        if condition is None:
+            action()
+        else:
+            pl.when(condition)(action)
+
+    barrier = pltpu.get_barrier_semaphore()
+    neighbours = [(has_left, at_left), (has_right, at_right)]
+    neighbours += [(exists, where) for exists, where, _, _ in bands]
+    for exists, where in neighbours:
+        when(exists, lambda: pl.semaphore_signal(barrier, inc=1, device_id=where, device_id_type=MESH))
+
     def load(source, target, slot):
         return pltpu.make_async_copy(source, target, local_sem.at[slot])
 
@@ -157,33 +193,6 @@
     loads += [load_first, load_second, load_back, load_inverse]
     for each in loads:
         each.start()
-
-    has_left, has_right = me_x > 0, me_x < xline_count - 1
-    at_left, at_right = {"xline": me_x - 1}, {"xline": me_x + 1}
-    if inline_count == 2:
-        bands = [(None, {"inline": 1 - me_i}, (1 - me_i) * (rows - HALF), 0)]
-        present = [None]
-    elif inline_count > 2:
-        has_above, has_below = me_i > 0, me_i < inline_count - 1
-        bands = [
-            (has_above, {"inline": me_i - 1}, 0, 1),
-            (has_below, {"inline": me_i + 1}, rows - HALF, 0),
-        ]
-        present = [has_above, has_below]
-    else:
-        bands, present = [], []
-
-    def when(condition, action):
-        if condition is None:
-            action()
-        else:
-            pl.when(condition)(action)
-
-    barrier = pltpu.get_barrier_semaphore()
-    neighbours = [(has_left, at_left), (has_right, at_right)]
-    neighbours += [(exists, where) for exists, where, _, _ in bands]
-    for exists, where in neighbours:
-        when(exists, lambda: pl.semaphore_signal(barrier, inc=1, device_id=where, device_id_type=MESH))
 
     def clear(*names):
         for name in names:
@@ -293,14 +302,14 @@
     for group in range(GROUPS):
         mine = slice(group * bins, (group + 1) * bins)
         pieces = [ordered[TAP_ROWS * piece : TAP_ROWS * (piece + 1), mine] for piece in range(4)]
-        response[group] = product(
+        response[group] = summed(
             taps_in[...], jnp.concatenate(pieces[:2], axis=1), jnp.concatenate(pieces[2:], axis=1)
         )
         if group < GROUPS - 1:
             forward_ends(group)
     load_first.wait()
     for group in range(GROUPS):
-        wave[group] = product(first_in[...], own_high[group], own_low[group])
+        wave[group] = summed(first_in[...], own_high[group], own_low[group])
         if group == 0:
             forward_ends(GROUPS - 1)
 
@@ -319,7 +328,7 @@
 
             when(exists, rest)
         high, low = parts(halo[group])
-        wave[group] += product(second_in[...], high, low)
+        wave[group] += summed(second_in[...], high, low)
 
         rc, rs = wave[group, :padded, :bins], wave[group, padded:, :bins]
         ic, js = wave[group, :padded, bins:], wave[group, padded:, bins:]
@@ -359,7 +368,7 @@
     sides = min(inline_count - 1, 2)
     places, around = layout(rows, cols, sides)
     own = rows * cols
-    waves = first.shape[0] // 2
+    waves = first.shape[0]
     lanes = 2 * frequencies // GROUPS
     tables = (forward, inverse, first, second, taps, back, order)
     operands = [traces.reshape(own, samples), filters.transpose(2, 0, 1)]

time: 16.6 us -> 16.3 us (0.982)
  Pallas kernels: 14.5 us -> 14.3 us
    pallas_call x1, Pallas kernels: 14.5 us -> 14.3 us  [per_device(): pl.pallas_call(functools.partial(kernel, rows, cols, inline_count, xline_...]
where the time goes in v5:
time: 16.3 us; the launch traced here: 16.2 us
  Pallas kernels  14.3 us (88%)
  local copies, waits for them, and re-layouts  1.89 us (12%)
    pallas_call x1, Pallas kernels, per_device(): pl.pallas_call(functools.partial(kernel, rows, cols, inline_count, xline_...  14.3 us
    unnamed x1, local copies, waits for them, and re-layouts  1.89 us

profile of v5, /device:TPU:1, one launch (start us, length us, event | category | flops | bytes accessed | tf_op | source)
XLA Modules:
  0.0 16.2 jit_solution(726423150233867747)
XLA Ops:
  0.0 14.3 %shard_map.91 = f32[128,1024]{1,0:T(8,128)} custom-call(f32[128,1024]{1,0:T(8,128)} %bitcast.4, f32[81,2,512]{2,1,0:T(2,128)} %bitcast.5, bf16[2,2,512,512]{3,2,1,0:T(8,128)(2,1)} %constant.14.clone.forward, bf16[2,2,512,512]{3,2,1,0:T(8,128)(2,1)} %constant.15.clone.inverse, bf16[416,384]{1,0:T(8,128)(2,1)} %constant.16.clone.first, ...), custom_call_target="tpu_custom_call" | custom-call | tf_op jit(solution)/shard_map/pallas_call | solution.py:377
  14.3 1.9 %copy.11 = f32[8,16,1024]{2,1,0:T(8,128)} copy(f32[8,16,1024]{2,1,0:T(8,128)} %bitcast.3) | data formatting | bytes 1048576

commit v6 on v5

--- a/solution.py
+++ b/solution.py
@@ -10,7 +10,7 @@
 from jax.sharding import PartitionSpec as P
 
 HALF = 4
-GROUPS = 2
+GROUPS = 4
 TAP_ROWS = 96
 MESH = pl.DeviceIdType.MESH
 BF16 = jnp.bfloat16

time: 16.3 us -> 16.8 us (1.031)
  Pallas kernels: 14.3 us -> 14.7 us
    pallas_call x1, Pallas kernels: 14.3 us -> 14.7 us  [per_device(): pl.pallas_call(functools.partial(kernel, rows, cols, inline_count, xline_...]
where the time goes in v6:
time: 16.8 us; the launch traced here: 16.6 us
  Pallas kernels  14.7 us (88%)
  local copies, waits for them, and re-layouts  1.89 us (11%)
    pallas_call x1, Pallas kernels, per_device(): pl.pallas_call(functools.partial(kernel, rows, cols, inline_count, xline_...  14.7 us
    unnamed x1, local copies, waits for them, and re-layouts  1.89 us

profile of v6, /device:TPU:1, one launch (start us, length us, event | category | flops | bytes accessed | tf_op | source)
XLA Modules:
  0.0 16.6 jit_solution(11365911444056921403)
XLA Ops:
  0.0 14.7 %shard_map.91 = f32[128,1024]{1,0:T(8,128)} custom-call(f32[128,1024]{1,0:T(8,128)} %bitcast.4, f32[81,2,512]{2,1,0:T(2,128)} %bitcast.5, bf16[2,4,512,256]{3,2,1,0:T(8,128)(2,1)} %constant.14.clone.forward, bf16[2,4,256,512]{3,2,1,0:T(8,128)(2,1)} %constant.15.clone.inverse, bf16[416,384]{1,0:T(8,128)(2,1)} %constant.16.clone.first, ...), custom_call_target="tpu_custom_call" | custom-call | tf_op jit(solution)/shard_map/pallas_call | solution.py:377
  14.7 1.9 %copy.11 = f32[8,16,1024]{2,1,0:T(8,128)} copy(f32[8,16,1024]{2,1,0:T(8,128)} %bitcast.3) | data formatting | bytes 1048576

commit v7 on v5

--- a/solution.py
+++ b/solution.py
@@ -12,6 +12,7 @@
 HALF = 4
 GROUPS = 2
 TAP_ROWS = 96
+PIECES = 4
 MESH = pl.DeviceIdType.MESH
 BF16 = jnp.bfloat16
 F32 = jnp.float32
@@ -261,7 +262,6 @@
             send(exists, remote(group, ("high", side), ends.at[group, 1, few], where))
         send(has_left, remote(group, "right", ends.at[group, 0], at_left))
         send(has_right, remote(group, "left", ends.at[group, 1], at_right))
-    for group in range(GROUPS):
         for exists, where, start, side in bands:
             many = pl.ds(pl.multiple_of(start * inner, HALF * inner), HALF * inner)
             send(exists, remote(group, ("middle", side), middle.at[group, many], where))
@@ -305,13 +305,10 @@
         response[group] = summed(
             taps_in[...], jnp.concatenate(pieces[:2], axis=1), jnp.concatenate(pieces[2:], axis=1)
         )
-        if group < GROUPS - 1:
-            forward_ends(group)
+    forward_ends(0)
     load_first.wait()
     for group in range(GROUPS):
         wave[group] = summed(first_in[...], own_high[group], own_low[group])
-        if group == 0:
-            forward_ends(GROUPS - 1)
 
     load_second.wait()
     load_back.wait()
@@ -344,6 +341,8 @@
             high, low = parts(value)
             kept[0, which * padded : (which + 1) * padded, part * bins : (part + 1) * bins] = high
             kept[1, which * padded : (which + 1) * padded, part * bins : (part + 1) * bins] = low
+        if group + 1 < GROUPS:
+            forward_ends(group + 1)
         filtered = product(back_in[...], kept[0], kept[1])
         filtered = jnp.concatenate(parts(filtered), axis=0)
         piece = product(filtered, inverse_in[0, group], inverse_in[1, group])
@@ -356,6 +355,19 @@
         when(condition, copy.wait_send)
     for group in range(GROUPS):
         sent_ends(group)
+
+
+def pass_on(rows, source, target, sem):
+    size = rows // PIECES
+    pieces = [pl.ds(piece * size, size) for piece in range(PIECES)]
+    copies = [
+        pltpu.make_async_copy(source.at[piece], target.at[piece], sem.at[slot])
+        for slot, piece in enumerate(pieces)
+    ]
+    for copy in copies:
+        copy.start()
+    for copy in copies:
+        copy.wait()
 
 
 def per_device(traces, filters, inline_count, xline_count):
@@ -407,6 +419,14 @@
             collective_id=0, has_side_effects=True, vmem_limit_bytes=60 * 1024 * 1024
         ),
     )(*operands)
+    result = pl.pallas_call(
+        functools.partial(pass_on, own),
+        out_shape=jax.ShapeDtypeStruct((own, samples), F32),
+        in_specs=[pl.BlockSpec(memory_space=pltpu.HBM)],
+        out_specs=pl.BlockSpec(memory_space=pltpu.HBM),
+        scratch_shapes=[pltpu.SemaphoreType.DMA((PIECES,))],
+        compiler_params=pltpu.CompilerParams(vmem_limit_bytes=60 * 1024 * 1024),
+    )(result)
     return result.reshape(rows, cols, samples)
 
 

time: 16.3 us -> 32.7 us (2.01)
  Pallas kernels: 14.3 us -> 32.5 us
  local copies, waits for them, and re-layouts: 1.89 us -> 0 us
    pallas_call x0 -> x1, Pallas kernels: none -> 17 us  [per_device(): pl.pallas_call(functools.partial(pass_on, own), out_shape=jax.ShapeDtypeS...]
    unnamed x1 -> x0, local copies, waits for them, and re-layouts: 1.89 us -> none
    pallas_call x1, Pallas kernels: 14.3 us -> 15.5 us  [per_device(): pl.pallas_call(functools.partial(kernel, rows, cols, inline_count, xline_...]
where the time goes in v7:
time: 32.7 us; the launch traced here: 32.5 us
  Pallas kernels  32.5 us (99%)
    pallas_call x1, Pallas kernels, per_device(): pl.pallas_call(functools.partial(pass_on, own), out_shape=jax.ShapeDtypeS...  17 us
    pallas_call x1, Pallas kernels, per_device(): pl.pallas_call(functools.partial(kernel, rows, cols, inline_count, xline_...  15.5 us

profile of v7, /device:TPU:1, one launch (start us, length us, event | category | flops | bytes accessed | tf_op | source)
XLA Modules:
  0.0 32.5 jit_solution(7137054934898350815)
XLA Ops:
  0.0 15.5 %shard_map.91.source = f32[128,1024]{1,0:T(8,128)} custom-call(f32[128,1024]{1,0:T(8,128)} %bitcast.3, f32[81,2,512]{2,1,0:T(2,128)} %bitcast.4, bf16[2,2,512,512]{3,2,1,0:T(8,128)(2,1)} %constant.14.clone.forward, bf16[2,2,512,512]{3,2,1,0:T(8,128)(2,1)} %constant.15.clone.inverse, bf16[416,384]{1,0:T(8,128)(2,1)} %constant.16.clone.first, ...), custom_call_target="tpu_custom_call" | custom-call | tf_op jit(solution)/shard_map/pallas_call | solution.py:389
  15.5 17.0 %shard_map.92 = f32[128,1024]{1,0:T(8,128)} custom-call(f32[128,1024]{1,0:T(8,128)} %shard_map.91.source), custom_call_target="tpu_custom_call" | custom-call | tf_op jit(solution)/shard_map/pallas_call | solution.py:422

commit v8 on v5

--- a/solution.py
+++ b/solution.py
@@ -132,7 +132,7 @@
 
 def kernel(
     rows, cols, inline_count, xline_count,
-    traces, filters, forward, inverse, first, second, taps, back, order,
+    traces, filters, temporal, spatial,
     out,
     own_in, own, own_high, own_low, ends, middle, halo, wave, response, kept, tap_rows,
     filters_in, forward_in, inverse_in, first_in, second_in, taps_in, back_in, order_in,
@@ -180,15 +180,26 @@
         return pltpu.make_async_copy(source, target, local_sem.at[slot])
 
     load_own = load(traces, own_in, 0)
-    load_forward = [load(forward.at[:, group], forward_in.at[:, group], 1 + group) for group in range(GROUPS)]
+    load_forward = [load(temporal.at[0, :, group], forward_in.at[:, group], 1 + group) for group in range(GROUPS)]
+    waves = wave.shape[1]
+
+    def table(start, target, slot):
+        count = target.shape[0]
+        return load(spatial.at[pl.ds(start, count)], target, slot)
+
     base = 1 + GROUPS
     load_filters = load(filters, filters_in, base)
-    load_order = load(order, order_in, base + 1)
-    load_taps = load(taps, taps_in, base + 2)
-    load_first = load(first, first_in, base + 3)
-    load_second = load(second.at[me_i if inline_count == 2 else 0], second_in, base + 4)
-    load_back = load(back, back_in, base + 5)
-    load_inverse = load(inverse, inverse_in, base + 6)
+    frequencies = order_in.shape[0]
+    load_order = table(0, order_in, base + 1)
+    load_taps = table(frequencies, taps_in, base + 2)
+    load_first = table(frequencies + waves, first_in, base + 3)
+    after = frequencies + 2 * waves
+    load_back = table(after, back_in, base + 5)
+    after += back_in.shape[0]
+    if inline_count == 2:
+        after = pl.multiple_of(after + me_i * waves, 16)
+    load_second = table(after, second_in, base + 4)
+    load_inverse = load(temporal.at[1], inverse_in, base + 6)
     loads = [load_own, *load_forward, load_filters, load_order, load_taps]
     loads += [load_first, load_second, load_back, load_inverse]
     for each in loads:
@@ -288,6 +299,7 @@
 
             when(exists, on)
 
+    forward_ends(0)
     load_filters.wait()
     load_order.wait()
     load_taps.wait()
@@ -297,19 +309,19 @@
         tap_rows[part, :tap_count, :] = filters_in[:, part, :]
     real, imag = parts(tap_rows[0]), parts(tap_rows[1])
     ordered = jnp.dot(
-        jnp.concatenate((real[0], imag[0], real[1], imag[1]), axis=0), order_in[...], preferred_element_type=F32
+        jnp.concatenate((real[0], imag[0], real[1], imag[1]), axis=0),
+        order_in[:, :frequencies],
+        preferred_element_type=F32
     ).astype(BF16)
     for group in range(GROUPS):
         mine = slice(group * bins, (group + 1) * bins)
         pieces = [ordered[TAP_ROWS * piece : TAP_ROWS * (piece + 1), mine] for piece in range(4)]
         response[group] = summed(
-            taps_in[...], jnp.concatenate(pieces[:2], axis=1), jnp.concatenate(pieces[2:], axis=1)
+            taps_in[:, : 3 * TAP_ROWS], jnp.concatenate(pieces[:2], axis=1), jnp.concatenate(pieces[2:], axis=1)
         )
-        if group < GROUPS - 1:
-            forward_ends(group)
     load_first.wait()
     for group in range(GROUPS):
-        wave[group] = summed(first_in[...], own_high[group], own_low[group])
+        wave[group] = summed(first_in[:, : 3 * rows * cols], own_high[group], own_low[group])
         if group == 0:
             forward_ends(GROUPS - 1)
 
@@ -328,7 +340,7 @@
 
             when(exists, rest)
         high, low = parts(halo[group])
-        wave[group] += summed(second_in[...], high, low)
+        wave[group] += summed(second_in[:, : 3 * halo.shape[1]], high, low)
 
         rc, rs = wave[group, :padded, :bins], wave[group, padded:, :bins]
         ic, js = wave[group, :padded, bins:], wave[group, padded:, bins:]
@@ -344,7 +356,7 @@
             high, low = parts(value)
             kept[0, which * padded : (which + 1) * padded, part * bins : (part + 1) * bins] = high
             kept[1, which * padded : (which + 1) * padded, part * bins : (part + 1) * bins] = low
-        filtered = product(back_in[...], kept[0], kept[1])
+        filtered = product(back_in[:, : 2 * padded], kept[0], kept[1])
         filtered = jnp.concatenate(parts(filtered), axis=0)
         piece = product(filtered, inverse_in[0, group], inverse_in[1, group])
         parity = group // (GROUPS // 2)
@@ -370,9 +382,11 @@
     own = rows * cols
     waves = first.shape[0]
     lanes = 2 * frequencies // GROUPS
-    tables = (forward, inverse, first, second, taps, back, order)
+    pieces = [order, taps, first, back, *second]
+    wide = -(-max(piece.shape[1] for piece in pieces) // 128) * 128
+    spatial = np.concatenate([np.pad(piece, ((0, 0), (0, wide - piece.shape[1]))) for piece in pieces])
     operands = [traces.reshape(own, samples), filters.transpose(2, 0, 1)]
-    operands += [jnp.asarray(table) for table in tables]
+    operands += [jnp.asarray(np.stack((forward, inverse))), jnp.asarray(spatial)]
     copies = GROUPS * len(places)
     result = pl.pallas_call(
         functools.partial(kernel, rows, cols, inline_count, xline_count),
@@ -394,17 +408,17 @@
             pltpu.VMEM((tap_count, 2, frequencies), F32),
             pltpu.VMEM(forward.shape, BF16),
             pltpu.VMEM(inverse.shape, BF16),
-            pltpu.VMEM(first.shape, BF16),
-            pltpu.VMEM(second.shape[1:], BF16),
-            pltpu.VMEM(taps.shape, BF16),
-            pltpu.VMEM(back.shape, BF16),
-            pltpu.VMEM(order.shape, BF16),
+            pltpu.VMEM((waves, wide), BF16),
+            pltpu.VMEM((waves, wide), BF16),
+            pltpu.VMEM((waves, wide), BF16),
+            pltpu.VMEM((back.shape[0], wide), BF16),
+            pltpu.VMEM((frequencies, wide), BF16),
             pltpu.SemaphoreType.DMA((8 + GROUPS,)),
             pltpu.SemaphoreType.DMA((copies,)),
             pltpu.SemaphoreType.DMA((copies,)),
         ],
         compiler_params=pltpu.CompilerParams(
-            collective_id=0, has_side_effects=True, vmem_limit_bytes=60 * 1024 * 1024
+            collective_id=0, has_side_effects=True, vmem_limit_bytes=53 * 1024 * 1024
         ),
     )(*operands)
     return result.reshape(rows, cols, samples)

time: 16.3 us -> 15.4 us (0.945)
  Pallas kernels: 14.3 us -> 13.5 us
    pallas_call x1, Pallas kernels: 14.3 us -> 13.5 us  [per_device(): pl.pallas_call(functools.partial(kernel, rows, cols, inline_count, xline_...]
    unnamed x1 -> x3, local copies, waits for them, and re-layouts: 1.89 us -> 1.77 us
where the time goes in v8:
time: 15.4 us; the launch traced here: 15.3 us
  Pallas kernels  13.5 us (88%)
  local copies, waits for them, and re-layouts  1.77 us (11%)
    pallas_call x1, Pallas kernels, per_device(): pl.pallas_call(functools.partial(kernel, rows, cols, inline_count, xline_...  13.5 us
    unnamed x3, local copies, waits for them, and re-layouts  1.77 us

profile of v8, /device:TPU:1, one launch (start us, length us, event | category | flops | bytes accessed | tf_op | source)
XLA Modules:
  0.0 15.3 jit_solution(18297523150978306542)
XLA Ops:
  0.0 0.0 copy-start
  0.0 1.0 %copy-done = f32[2,512,81]{1,0,2:T(2,128)S(1)} copy-done((f32[2,512,81]{1,0,2:T(2,128)S(1)}, f32[2,512,81]{1,0,2:T(2,128)}, u32[]{:S(2)}) %copy-start) | copy-done | bytes 331800
  1.0 13.5 %shard_map.46 = f32[128,1024]{1,0:T(8,128)S(1)} custom-call(f32[128,1024]{1,0:T(8,128)} %bitcast.5, f32[81,2,512]{2,1,0:T(2,128)S(1)} %bitcast.4, bf16[2,2,2,512,512]{4,3,2,1,0:T(8,128)(2,1)} %constant.4.clone.temporal, bf16[2432,512]{1,0:T(8,128)(2,1)} %constant.5.clone.spatial), custom_call_target="tpu_custom_call" | custom-call | tf_op jit(solution)/shard_map/pallas_call | solution.py:391
  14.5 0.8 %copy.6 = f32[8,16,1024]{2,1,0:T(8,128)} copy(f32[8,16,1024]{2,1,0:T(8,128)S(1)} %bitcast.3) | data formatting | bytes 1048576
Async XLA Ops:
  0.0 1.0 %copy-start = (f32[2,512,81]{1,0,2:T(2,128)S(1)}, f32[2,512,81]{1,0,2:T(2,128)}, u32[]{:S(2)}) copy-start(f32[2,512,81]{1,0,2:T(2,128)} %param.5) | copy-start | bytes 995332

commit v9 on v8

--- a/solution.py
+++ b/solution.py
@@ -319,11 +319,11 @@
         response[group] = summed(
             taps_in[:, : 3 * TAP_ROWS], jnp.concatenate(pieces[:2], axis=1), jnp.concatenate(pieces[2:], axis=1)
         )
+        if group < GROUPS - 1:
+            forward_ends(group + 1)
     load_first.wait()
     for group in range(GROUPS):
         wave[group] = summed(first_in[:, : 3 * rows * cols], own_high[group], own_low[group])
-        if group == 0:
-            forward_ends(GROUPS - 1)
 
     load_second.wait()
     load_back.wait()

time: 15.4 us -> 15.4 us (level)
  no operation moved by 1% of the time
where the time goes in v9:
time: 15.4 us; the launch traced here: 15.3 us
  Pallas kernels  13.5 us (88%)
  local copies, waits for them, and re-layouts  1.77 us (11%)
    pallas_call x1, Pallas kernels, per_device(): pl.pallas_call(functools.partial(kernel, rows, cols, inline_count, xline_...  13.5 us
    unnamed x3, local copies, waits for them, and re-layouts  1.77 us

profile of v9, /device:TPU:1, one launch (start us, length us, event | category | flops | bytes accessed | tf_op | source)
XLA Modules:
  0.0 15.3 jit_solution(16543991637993348250)
XLA Ops:
  0.0 0.0 copy-start
  0.0 1.0 %copy-done = f32[2,512,81]{1,0,2:T(2,128)S(1)} copy-done((f32[2,512,81]{1,0,2:T(2,128)S(1)}, f32[2,512,81]{1,0,2:T(2,128)}, u32[]{:S(2)}) %copy-start) | copy-done | bytes 331800
  1.0 13.5 %shard_map.46 = f32[128,1024]{1,0:T(8,128)S(1)} custom-call(f32[128,1024]{1,0:T(8,128)} %bitcast.5, f32[81,2,512]{2,1,0:T(2,128)S(1)} %bitcast.4, bf16[2,2,2,512,512]{4,3,2,1,0:T(8,128)(2,1)} %constant.4.clone.temporal, bf16[2432,512]{1,0:T(8,128)(2,1)} %constant.5.clone.spatial), custom_call_target="tpu_custom_call" | custom-call | tf_op jit(solution)/shard_map/pallas_call | solution.py:391
  14.5 0.8 %copy.6 = f32[8,16,1024]{2,1,0:T(8,128)} copy(f32[8,16,1024]{2,1,0:T(8,128)S(1)} %bitcast.3) | data formatting | bytes 1048576
Async XLA Ops:
  0.0 1.0 %copy-start = (f32[2,512,81]{1,0,2:T(2,128)S(1)}, f32[2,512,81]{1,0,2:T(2,128)}, u32[]{:S(2)}) copy-start(f32[2,512,81]{1,0,2:T(2,128)} %param.5) | copy-start | bytes 995332

commit v10 on v9

--- a/solution.py
+++ b/solution.py
@@ -84,6 +84,10 @@
         places[name] = (at, size)
         at += size
     return places, at
+
+
+def early_count(rows, sides):
+    return 2 * rows * HALF + (2 * HALF * HALF if sides == 1 else 0)
 
 
 def spatial_tables(rows, cols, inline_count):
@@ -103,7 +107,10 @@
             places += grid(band, range(HALF)) + grid(band, range(cols - HALF, cols))
             places += grid(band, range(HALF, cols - HALF))
             places += grid(band, below_zero) + grid(band, above_end)
-        second.append(thrice(basis(places)))
+        soon = early_count(rows, sides)
+        early, late = thrice(basis(places[:soon])), thrice(basis(places[soon:]))
+        early = np.pad(early, ((0, 0), (0, -early.shape[1] % 128)))
+        second.append(np.concatenate((early, late), axis=1))
     reach = range(-HALF, HALF + 1)
     taps = np.zeros((2 * padded, TAP_ROWS))
     taps[:, : len(reach) ** 2] = basis(grid(reach, reach))
@@ -322,16 +329,22 @@
         if group < GROUPS - 1:
             forward_ends(group + 1)
     load_first.wait()
+    load_second.wait()
+    soon = early_count(rows, sides)
+    late_at = -(-3 * soon // 128) * 128
+    late = halo.shape[1] - soon
     for group in range(GROUPS):
         wave[group] = summed(first_in[:, : 3 * rows * cols], own_high[group], own_low[group])
-
-    load_second.wait()
+    for group in range(GROUPS):
+        pl.when(has_left)(lambda: come(group, "left"))
+        pl.when(has_right)(lambda: come(group, "right"))
+        high, low = parts(halo[group, :soon])
+        wave[group] += summed(second_in[:, : 3 * soon], high, low)
+
     load_back.wait()
     load_inverse.wait()
     halfway = [None, None]
     for group in range(GROUPS):
-        pl.when(has_left)(lambda: come(group, "left"))
-        pl.when(has_right)(lambda: come(group, "right"))
         for side, exists in enumerate(present):
             def rest(side=side):
                 come(group, ("middle", side))
@@ -339,8 +352,9 @@
                 pl.when(has_right)(lambda: come(group, ("from_right", side)))
 
             when(exists, rest)
-        high, low = parts(halo[group])
-        wave[group] += summed(second_in[:, : 3 * halo.shape[1]], high, low)
+        if late:
+            high, low = parts(halo[group, soon:])
+            wave[group] += summed(second_in[:, late_at : late_at + 3 * late], high, low)
 
         rc, rs = wave[group, :padded, :bins], wave[group, padded:, :bins]
         ic, js = wave[group, :padded, bins:], wave[group, padded:, bins:]

time: 15.4 us -> 15.2 us (0.987)
  Pallas kernels: 13.5 us -> 13.3 us
    pallas_call x1, Pallas kernels: 13.5 us -> 13.3 us  [per_device(): pl.pallas_call(functools.partial(kernel, rows, cols, inline_count, xline_...]
where the time goes in v10:
time: 15.2 us; the launch traced here: 15.1 us
  Pallas kernels  13.3 us (88%)
  local copies, waits for them, and re-layouts  1.77 us (12%)
    pallas_call x1, Pallas kernels, per_device(): pl.pallas_call(functools.partial(kernel, rows, cols, inline_count, xline_...  13.3 us
    unnamed x3, local copies, waits for them, and re-layouts  1.77 us

profile of v10, /device:TPU:1, one launch (start us, length us, event | category | flops | bytes accessed | tf_op | source)
XLA Modules:
  0.0 15.1 jit_solution(987895993237206538)
XLA Ops:
  0.0 0.0 copy-start
  0.0 1.0 %copy-done = f32[2,512,81]{1,0,2:T(2,128)S(1)} copy-done((f32[2,512,81]{1,0,2:T(2,128)S(1)}, f32[2,512,81]{1,0,2:T(2,128)}, u32[]{:S(2)}) %copy-start) | copy-done | bytes 331800
  1.0 13.3 %shard_map.46 = f32[128,1024]{1,0:T(8,128)S(1)} custom-call(f32[128,1024]{1,0:T(8,128)} %bitcast.5, f32[81,2,512]{2,1,0:T(2,128)S(1)} %bitcast.4, bf16[2,2,2,512,512]{4,3,2,1,0:T(8,128)(2,1)} %constant.4.clone.temporal, bf16[2432,640]{1,0:T(8,128)(2,1)} %constant.5.clone.spatial), custom_call_target="tpu_custom_call" | custom-call | tf_op jit(solution)/shard_map/pallas_call | solution.py:405
  14.3 0.8 %copy.6 = f32[8,16,1024]{2,1,0:T(8,128)} copy(f32[8,16,1024]{2,1,0:T(8,128)S(1)} %bitcast.3) | data formatting | bytes 1048576
Async XLA Ops:
  0.0 1.0 %copy-start = (f32[2,512,81]{1,0,2:T(2,128)S(1)}, f32[2,512,81]{1,0,2:T(2,128)}, u32[]{:S(2)}) copy-start(f32[2,512,81]{1,0,2:T(2,128)} %param.5) | copy-start | bytes 995332
